TPU v7x, 256 devices: a whole 4x4x8 slice. The times are simulated.
256 devices in a mesh: lat: 16 (over y, x_lo, core), lon: 16 (over z, x_hi).
Axes of the slice: x: 4 (x_hi: 2, x_lo: 2; x = x_hi * 2 + x_lo), y: 4, z: 8, core: 2. Of those that a mesh axis runs over, the one named last changes fastest.
Arguments:
- fields: bfloat16 [2, 288, 192, 512], P(None, 'lat', 'lon'), may hold values from -8 to 8
- tangent_pick: int32 [2, 288, 192], P(None, 'lat', 'lon'), may hold values from 0 to 511
- key_mask: int32 [2, 288, 192], P(None, 'lat', 'lon'), may hold values 0 or 1
- w_qkv: bfloat16 [2, 512, 1536], P(None, 'lon'), may hold values from -0.25 to 0.25
- w_out: bfloat16 [2, 512, 512], P(None, 'lon'), may hold values from -0.25 to 0.25
- w_up: bfloat16 [2, 512, 2048], P(None, 'lon'), may hold values from -0.25 to 0.25
- w_down: bfloat16 [2, 2048, 512], P(None, 'lon'), may hold values from -0.125 to 0.125
Outputs:
- primal_out: bfloat16 [2, 288, 192, 512], P(None, 'lat', 'lon')
- tangent_out: bfloat16 [2, 288, 192, 512], P(None, 'lat', 'lon')
All inputs are finite; a program needn't handle non-finite values. No bound on the sum of `key_mask` on one device may be relied on, other than what follows from the above.
Results may differ from a plain program's by a relative error of at most 0.03.
Values may be sent and summed in bfloat16 or wider, within the bound.
A program may use at most 128 MiB of HBM per device.

v0:
```python
import jax
import jax.numpy as jnp
from jax import lax
from jax.sharding import PartitionSpec as P

HEADS = 8
WLAT = 6
WLON = 12


norm_epsilon = 1e-05


def from_behind(x, axis, by):
    length = lax.axis_size(axis)
    return lax.ppermute(x, axis, [(i, (i + by) % length) for i in range(length)])


def joined_along(pieces, dim):
    pieces = jnp.moveaxis(pieces, 0, dim)
    dims = pieces.shape
    return pieces.reshape(*dims[:dim], dims[dim] * dims[dim + 1], *dims[dim + 2 :])


def gather_packed(arrays, axis, dims):
    flat = jnp.concatenate([a.reshape(-1) for a in arrays])
    lines, at, finished = (lax.all_gather(flat, axis), 0, [])
    for a, dim in zip(arrays, dims):
        pieces = lines[:, at : at + a.size].reshape(-1, *a.shape)
        finished.append(joined_along(pieces, dim))
        at += a.size
    return tuple(finished)


def layer_norm(values):
    center = jnp.mean(values, -1, keepdims=True)
    spread = jnp.mean(jnp.square(values - center), -1, keepdims=True)
    return (values - center) * lax.rsqrt(spread + norm_epsilon)


def window_attention(packed, usable, region):
    windows, window_len, triple = packed.shape
    model_width = triple // 3
    head_size = model_width // HEADS
    queries = packed[..., :model_width].reshape(windows, window_len, HEADS, head_size)
    keys_all = packed[..., model_width : 2 * model_width].reshape(
        windows, window_len, HEADS, head_size
    )
    values_all = packed[..., 2 * model_width :].reshape(windows, window_len, HEADS, head_size)
    scores = jnp.einsum(
        "wqhe,wkhe->whqk", queries, keys_all, preferred_element_type=jnp.float32
    ) * head_size ** (-0.5)
    matched = region[:, :, None] == region[:, None, :]
    allowed = (usable[:, None, :] > 0) & matched
    self_pair = jnp.eye(window_len, dtype=bool)
    allowed = allowed | self_pair[None]
    scores = jnp.where(allowed[:, None], scores, -1000000000.0)
    highest = lax.stop_gradient(jnp.max(scores, -1, keepdims=True))
    raised = jnp.exp(scores - highest)
    probs = (raised / jnp.sum(raised, -1, keepdims=True)).astype(jnp.bfloat16)
    mixed = jnp.einsum("whqk,wkhe->wqhe", probs, values_all, preferred_element_type=jnp.float32)
    return mixed.astype(jnp.bfloat16).reshape(windows, window_len, model_width)


def to_windows(array):
    levels, lat_rows, lon_cols = array.shape[:3]
    trailing = array.shape[3:]
    shaped = array.reshape((levels, lat_rows // WLAT, WLAT, lon_cols) + trailing)
    return jnp.moveaxis(shaped, 1, 0).reshape(
        (lat_rows // WLAT, levels * WLAT * lon_cols) + trailing
    )


def from_windows(flat_tokens, levels, lat_rows, lon_cols):
    shaped = flat_tokens.reshape(lat_rows // WLAT, levels, WLAT, lon_cols, -1)
    return jnp.moveaxis(shaped, 0, 1).reshape(levels, lat_rows, lon_cols, -1)


def direct(streams, complete):
    return (
        jnp.dot(streams[0], complete, preferred_element_type=jnp.float32),
        jnp.dot(streams[1], complete, preferred_element_type=jnp.float32),
    )


def linear_qkv(streams, complete):
    return direct(streams, complete)


def linear_out(streams, complete):
    return direct(streams, complete)


def linear_up(streams, complete):
    return direct(streams, complete)


def linear_down(streams, complete):
    return direct(streams, complete)


def advance(streams, arrived, cut, axis):
    return tuple(
        (
            jnp.concatenate(
                [lax.slice_in_dim(resident, cut, resident.shape[axis], axis=axis), incoming], axis
            )
            for resident, incoming in zip(streams, arrived)
        )
    )


def shift_ahead(primal, tangent, usable):
    half_lat = WLAT // 2
    half_lon = WLON // 2
    streams = (primal, tangent, usable)
    arrived = from_behind(
        (primal[:, :, :half_lon], tangent[:, :, :half_lon], usable[:, :, :half_lon]), "lon", -1
    )
    streams = advance(streams, arrived, half_lon, 2)
    primal, tangent, usable = streams
    arrived = from_behind(
        (primal[:, :half_lat], tangent[:, :half_lat], usable[:, :half_lat]), "lat", -1
    )
    streams = advance(streams, arrived, half_lat, 1)
    return streams


def shift_back(primal, tangent):
    lat_rows = primal.shape[1]
    lon_cols = primal.shape[2]
    lon_cut = lon_cols - WLON // 2
    arrived = from_behind((primal[:, :, lon_cut:], tangent[:, :, lon_cut:]), "lon", 1)
    primal = jnp.concatenate([arrived[0], primal[:, :, :lon_cut]], 2)
    tangent = jnp.concatenate([arrived[1], tangent[:, :, :lon_cut]], 2)
    lat_cut = lat_rows - WLAT // 2
    arrived = from_behind((primal[:, lat_cut:], tangent[:, lat_cut:]), "lat", 1)
    primal = jnp.concatenate([arrived[0], primal[:, :lat_cut]], 1)
    tangent = jnp.concatenate([arrived[1], tangent[:, :lat_cut]], 1)
    return (primal, tangent)


def run_block(primal, tangent, usable, region, complete):
    levels, lat_rows, lon_cols, model_width = primal.shape
    streams = (
        to_windows(primal).reshape(-1, model_width),
        to_windows(tangent).reshape(-1, model_width),
    )
    usable_w = to_windows(usable)
    region_w = to_windows(region)
    windows = usable_w.shape[0]
    packed = linear_qkv(streams, complete[0])
    packed = (packed[0].astype(jnp.bfloat16), packed[1].astype(jnp.bfloat16))

    def attend(values):
        return window_attention(
            values.reshape(windows, -1, 3 * model_width), usable_w, region_w
        ).reshape(-1, model_width)

    attended = jax.jvp(attend, (packed[0],), (packed[1],))
    projected = linear_out(attended, complete[1])

    def post_attention(residual_in, branch):
        return residual_in.astype(jnp.float32) + layer_norm(branch)

    hidden = jax.jvp(post_attention, (streams[0], projected[0]), (streams[1], projected[1]))
    up_proj = linear_up(
        (hidden[0].astype(jnp.bfloat16), hidden[1].astype(jnp.bfloat16)), complete[2]
    )

    def activate(values):
        return jax.nn.gelu(values, approximate=False).astype(jnp.bfloat16)

    activated = jax.jvp(activate, (up_proj[0],), (up_proj[1],))
    down_proj = linear_down(activated, complete[3])

    def post_mlp(residual_in, branch):
        return (residual_in + layer_norm(branch)).astype(jnp.bfloat16)

    result = jax.jvp(post_mlp, (hidden[0], down_proj[0]), (hidden[1], down_proj[1]))
    return (
        from_windows(result[0], levels, lat_rows, lon_cols),
        from_windows(result[1], levels, lat_rows, lon_cols),
    )


def on_device(fields, tangent_pick, key_mask, w_qkv, w_out, w_up, w_down):
    levels, lat_rows, lon_cols, model_width = fields.shape
    primal = fields
    tangent = jax.nn.one_hot(tangent_pick, model_width, dtype=jnp.bfloat16)
    usable = key_mask.astype(jnp.bfloat16)
    for block_index in range(2):
        complete = gather_packed(
            (w_qkv[block_index], w_out[block_index], w_up[block_index], w_down[block_index]),
            "lon",
            (0, 0, 0, 0),
        )
        region = jnp.zeros((levels, lat_rows, lon_cols), jnp.int32)
        if block_index == 1:
            primal, tangent, usable = shift_ahead(primal, tangent, usable)
            at_edge = lax.axis_index("lat") == lax.axis_size("lat") - 1
            row_ids = lax.broadcasted_iota(jnp.int32, (levels, lat_rows, lon_cols), 1)
            region = ((row_ids >= lat_rows - WLAT // 2) & at_edge).astype(jnp.int32)
        primal, tangent = run_block(primal, tangent, usable, region, complete)
        if block_index == 1:
            primal, tangent = shift_back(primal, tangent)
    return (primal, tangent)


def solution(mesh):
    in_specs = (
        P(None, "lat", "lon", None),
        P(None, "lat", "lon"),
        P(None, "lat", "lon"),
        P(None, "lon", None),
        P(None, "lon", None),
        P(None, "lon", None),
        P(None, "lon", None),
    )
    out_specs = (P(None, "lat", "lon", None), P(None, "lat", "lon", None))
    return jax.shard_map(
        on_device, mesh=mesh, in_specs=in_specs, out_specs=out_specs, check_vma=False
    )
```

profile of v0, /device:TPU:64, one launch (start us, length us, event | category | flops | bytes accessed | tf_op | source)
XLA Modules:
  0.0 376.9 jit_solution(14326063626545188965)
XLA Ops:
  12.2 2.6 collective-permute-start.2
  17.4 2.3 collective-permute-start.3
  22.3 107.5 %all-gather.5.cloned.1.call-done = bf16[3145728]{0:T(1024)(128)(2,1)} async-done(((bf16[196608]{0:T(1024)(128)(2,1)}), bf16[3145728]{0:T(1024)(128)(2,1)}) %all-gather.5.cloned.1.call-update) | async-done | bytes 6291472 | tf_op jit(solution)/shard_map/all_gather | solution.py:27
  129.8 6.6 %reshape.335 = bf16[16,196608]{1,0:T(8,128)(2,1)} reshape(bf16[3145728]{0:T(1024)(128)(2,1)} %all-gather.5.cloned.1.call-done) | data formatting | bytes 12582912 | tf_op jit(solution)/shard_map/all_gather | solution.py:27
  136.3 4.5 %fusion.83 = (bf16[16,65536]{1,0:T(8,128)(2,1)}, bf16[16,65536]{1,0:T(8,128)(2,1)}) fusion(bf16[16,196608]{1,0:T(8,128)(2,1)} %reshape.335), kind=kLoop, calls=%fused_computation.176 | loop fusion | bytes 8388608 | tf_op jit(solution)/shard_map/slice | solution.py:29
  142.3 1.6 reshape_reshape.35
  144.0 2.3 convolution_convert_fusion
  153.6 2.0 fusion.111
  155.7 5.2 %fusion.95 = (f32[3,8,144]{2,1,0:T(8,128)}, f32[3,8,144,144]{2,3,1,0:T(8,128)}) fusion(pred[3,144,144]{1,2,0:T(8,128)(4,1)} %get-tuple-element.49, bf16[3,144,8,64]{1,3,2,0:T(8,128)(2,1)} %bitcast.126, bf16[3,144,8,64]{1,3,2,0:T(8,128)(2,1)} %bitcast.129), kind=kOutput, calls=%fused_computation.188 | convolution fusion | flops 65691792 | bytes 2951424 | tf_op jit(solution)/shard_map/jvp()/sub | solution.py:59
  160.9 5.4 %fusion.96 = (f32[3,8,144]{2,1,0:T(8,128)S(1)}, f32[3,8,144,144]{2,3,1,0:T(8,128)}) fusion(f32[3,8,144,144]{2,3,1,0:T(8,128)} %get-tuple-element.61, f32[3,8,144,144]{2,3,1,0:T(8,128)S(1)} %fusion.111, bf16[3,144,8,64]{1,3,2,0:T(8,128)(2,1)} %bitcast.127, bf16[3,144,8,64]{1,3,2,0:T(8,128)(2,1)} %bitcast.133, pred[3,144,144]{1,2,0:T(8,128)(4,1)} %get-tuple-element.49), kind=kOutput, calls=%fused_computation.189 | convolution fusion | flops 66185856 | bytes 6932736 | tf_op jit(solution)/shard_map/jvp(wqhe,wkhe->whqk)/dot_general | solution.py:50
  166.2 2.2 copy.102
  170.6 2.4 divide_convert_fusion.1
  173.0 3.9 %fusion.26 = f32[3,8,64,144]{3,2,1,0:T(8,128)S(1)} fusion(bf16[3,144,8,64]{1,3,2,0:T(8,128)(2,1)S(1)} %bitcast.140, f32[3,8,144,144]{2,3,1,0:T(8,128)} %get-tuple-element.61, f32[3,8,144,144]{2,3,1,0:T(8,128)} %get-tuple-element.63, f32[3,8,144]{2,1,0:T(8,128)S(1)} %multiply_divide_fusion.1, f32[3,8,144]{2,1,0:T(8,128)S(1)} %neg.32, ...), kind=kOutput, calls=%fused_computation.62 | convolution fusion | flops 66189312 | bytes 5349888 | tf_op jit(solution)/shard_map/jvp(whqk,wkhe->wqhe)/dot_general | solution.py:61
  178.2 2.1 copy.127
  181.9 2.5 fusion.30
  184.4 2.2 copy.108
  187.9 2.0 reshape_reshape.37
  189.9 11.1 %reshape_reshape.38 = bf16[2048,512]{1,0:T(8,128)(2,1)S(1)} reshape(bf16[16,65536]{1,0:T(8,128)(2,1)} %get-tuple-element.13) | data formatting | bytes 4194304 | tf_op jit(solution)/shard_map/reshape;reshape | solution.py:22
  203.0 7.8 %fusion.2 = (f32[432,2048]{1,0:T(8,128)S(1)}, f32[432,2048]{1,0:T(8,128)S(1)}) fusion(bf16[512,2048]{1,0:T(8,128)(2,1)S(1)} %copy-done.17, f32[432,512]{1,0:T(8,128)S(1)} %get-tuple-element.67, bf16[432,512]{1,0:T(8,128)(2,1)S(1)} %copy-done.19, f32[432]{0:T(512)S(1)} %get-tuple-element.59, f32[432]{0:T(512)S(1)} %get-tuple-element.89), kind=kOutput, calls=%fused_computation.4 | convolution fusion | flops 961929216 | bytes 10505600 | tf_op jit(solution)/shard_map/dot_general | solution.py:81
  213.9 8.0 %fusion.99 = (f32[432]{0:T(512)S(1)}, f32[432,512]{1,0:T(8,128)}) fusion(bf16[2048,512]{1,0:T(8,128)(2,1)S(1)} %reshape_reshape.38, f32[432,2048]{1,0:T(8,128)} %copy-done.1, f32[432,2048]{1,0:T(8,128)} %copy-done.2, bf16[512,2048]{1,0:T(8,128)(2,1)} %reshape_reshape.37, f32[432,512]{1,0:T(8,128)} %copy-done.9, f32[432,512]{1,0:T(8,128)} %copy-done.10, ...), kind=kOutput, calls=%fused_computation.192 | convolution fusion | flops 1826758272 | bytes 13936768 | tf_op jit(solution)/shard_map/dot_general | solution.py:82
  221.8 1.6 multiply_reduce_fusion.2
  223.5 2.1 add_convert_fusion.11
  229.3 3.0 collective-permute-start
  232.3 22.1 %all-gather.7.cloned.1.call-done = bf16[3145728]{0:T(1024)(128)(2,1)} async-done(((bf16[196608]{0:T(1024)(128)(2,1)}), bf16[3145728]{0:T(1024)(128)(2,1)}) %all-gather.7.cloned.1.call-update) | async-done | bytes 6291472 | tf_op jit(solution)/shard_map/all_gather | solution.py:27
  254.4 6.2 %reshape.336 = bf16[16,196608]{1,0:T(8,128)(2,1)} reshape(bf16[3145728]{0:T(1024)(128)(2,1)} %all-gather.7.cloned.1.call-done) | data formatting | bytes 12582912 | tf_op jit(solution)/shard_map/all_gather | solution.py:27
  260.7 4.5 %fusion.84 = (bf16[16,65536]{1,0:T(8,128)(2,1)}, bf16[16,65536]{1,0:T(8,128)(2,1)}) fusion(bf16[16,196608]{1,0:T(8,128)(2,1)} %reshape.336), kind=kLoop, calls=%fused_computation.177 | loop fusion | bytes 8388608 | tf_op jit(solution)/shard_map/slice | solution.py:29
  266.5 1.7 reshape_reshape.40
  268.4 3.4 reshape_reshape.42
  271.8 1.9 reshape_reshape.43
  275.1 1.9 collective-permute-start.1
  279.7 2.4 convolution_convert_fusion.1
  284.3 2.4 convolution_convert_fusion.3
  289.4 3.9 %fusion.112 = f32[3,8,144,144]{2,3,1,0:T(8,128)} fusion(bf16[3,144,8,64]{1,3,2,0:T(8,128)(2,1)S(1)} %bitcast.125, bf16[3,144,8,64]{1,3,2,0:T(8,128)(2,1)} %bitcast.136), kind=kOutput, calls=%fused_computation.201 | convolution fusion | flops 63700992 | bytes 2875392 | tf_op jit(solution)/shard_map/jvp(wqhe,wkhe->whqk)/dot_general | solution.py:50
  293.3 4.3 %fusion.103 = (f32[3,8,144]{2,1,0:T(8,128)S(1)}, f32[3,8,144,144]{2,3,1,0:T(8,128)}) fusion(pred[3,144,144]{1,2,0:T(8,128)(4,1)S(1)} %copy-done.29, bf16[3,144,8,64]{1,3,2,0:T(8,128)(2,1)S(1)} %bitcast.131, bf16[3,144,8,64]{1,3,2,0:T(8,128)(2,1)} %bitcast.137), kind=kOutput, calls=%fused_computation.194 | convolution fusion | flops 65691792 | bytes 2951424 | tf_op jit(solution)/shard_map/jvp()/sub | solution.py:59
  297.6 2.5 divide_convert_fusion
  300.9 4.9 %fusion.104 = (f32[3,8,144]{2,1,0:T(8,128)S(1)}, f32[3,8,144,144]{2,3,1,0:T(8,128)}) fusion(f32[3,8,144,144]{2,3,1,0:T(8,128)} %get-tuple-element.75, f32[3,8,144,144]{2,3,1,0:T(8,128)S(1)} %copy-done, bf16[3,144,8,64]{1,3,2,0:T(8,128)(2,1)S(1)} %bitcast.132, bf16[3,144,8,64]{1,3,2,0:T(8,128)(2,1)S(1)} %bitcast.130, pred[3,144,144]{1,2,0:T(8,128)(4,1)S(1)} %copy-done.29), kind=kOutput, calls=%fused_computation.195 | convolution fusion | flops 66185856 | bytes 6932736 | tf_op jit(solution)/shard_map/jvp(wqhe,wkhe->whqk)/dot_general | solution.py:50
  305.8 2.2 copy.111
  309.2 2.5 fusion.31
  311.7 4.1 %fusion.27 = f32[3,8,64,144]{3,2,1,0:T(8,128)S(1)} fusion(bf16[3,144,8,64]{1,3,2,0:T(8,128)(2,1)} %bitcast.142, f32[3,8,144,144]{2,3,1,0:T(8,128)} %get-tuple-element.75, f32[3,8,144,144]{2,3,1,0:T(8,128)} %get-tuple-element.77, f32[3,8,144]{2,1,0:T(8,128)S(1)} %multiply_divide_fusion, f32[3,8,144]{2,1,0:T(8,128)S(1)} %neg.34, ...), kind=kOutput, calls=%fused_computation.63 | convolution fusion | flops 66189312 | bytes 5349888 | tf_op jit(solution)/shard_map/jvp(whqk,wkhe->wqhe)/dot_general | solution.py:61
  317.1 2.2 copy.135
  324.1 9.0 %fusion.3 = (f32[432,2048]{1,0:T(8,128)S(1)}, f32[432,2048]{1,0:T(8,128)S(1)}) fusion(bf16[512,2048]{1,0:T(8,128)(2,1)S(1)} %copy-done.16, f32[432,512]{1,0:T(8,128)S(1)} %get-tuple-element.81, bf16[432,512]{1,0:T(8,128)(2,1)} %copy-done.26, f32[432]{0:T(512)S(1)} %get-tuple-element.55, f32[432]{0:T(512)S(1)} %broadcast_multiply_fusion.5), kind=kOutput, calls=%fused_computation.5 | convolution fusion | flops 961929216 | bytes 10505600 | tf_op jit(solution)/shard_map/dot_general | solution.py:81
  336.0 7.9 %fusion.107 = (f32[432]{0:T(512)S(1)}, f32[432,512]{1,0:T(8,128)}) fusion(bf16[2048,512]{1,0:T(8,128)(2,1)S(1)} %copy-done.5, f32[432,2048]{1,0:T(8,128)} %copy-done.3, f32[432,2048]{1,0:T(8,128)} %copy-done.4, bf16[512,2048]{1,0:T(8,128)(2,1)} %reshape_reshape.42, bf16[432,512]{1,0:T(8,128)(2,1)S(1)} %copy-done.25, f32[432,512]{1,0:T(8,128)} %copy-done.8, ...), kind=kOutput, calls=%fused_computation.198 | convolution fusion | flops 1826315904 | bytes 14377408 | tf_op jit(solution)/shard_map/dot_general | solution.py:82
  343.8 1.6 multiply_reduce_fusion
  345.5 2.3 add_convert_fusion.10
  349.6 4.7 %collective-permute-start.4 = (bf16[2,18,6,512]{3,0,2,1:T(2,128)(2,1)S(1)}, bf16[2,18,6,512]{3,0,2,1:T(2,128)(2,1)S(1)}, u32[]{:S(2)}, u32[]{:S(2)}) collective-permute-start(bf16[2,18,6,512]{3,0,2,1:T(2,128)(2,1)S(1)} %get-tuple-element.34), channel_id=1, source_target_pairs={{0,1},{1,2},{2,3},{3,4},{4,5},{5,6},{6,7},{7,8},{8,9},{9,10},{10,1... | collective-permute-start | bytes 663560 | tf_op jit(solution)/shard_map/ppermute | solution.py:16
  354.3 5.1 %collective-permute-done.8 = bf16[2,18,6,512]{3,0,2,1:T(2,128)(2,1)S(1)} collective-permute-done((bf16[2,18,6,512]{3,0,2,1:T(2,128)(2,1)S(1)}, bf16[2,18,6,512]{3,0,2,1:T(2,128)(2,1)S(1)}, u32[]{:S(2)}, u32[]{:S(2)}) %collective-permute-start.8) | collective-permute-done | bytes 221216 | tf_op jit(solution)/shard_map/ppermute | solution.py:16
  359.7 2.7 collective-permute-done.4
  362.6 3.0 collective-permute-done.9
  (204 shorter events, 61.5 us)
Async XLA Ops:
  7.2 5.0 %copy-start.32 = (s32[2,18,12]{1,0,2:T(2,128)S(1)}, s32[2,18,12]{1,0,2:T(2,128)}, u32[]{:S(2)}) copy-start(s32[2,18,12]{1,0,2:T(2,128)} %param.9) | copy-start | bytes 5188
  7.2 8.7 %copy-start.33 = (s32[2,18,12]{1,0,2:T(2,128)S(1)}, s32[2,18,12]{1,0,2:T(2,128)}, u32[]{:S(2)}) copy-start(s32[2,18,12]{1,0,2:T(2,128)} %param.8) | copy-start | bytes 5188
  7.2 9.6 %copy-start.30 = (bf16[2,18,12,512]{3,0,2,1:T(2,128)(2,1)S(1)}, bf16[2,18,12,512]{3,0,2,1:T(2,128)(2,1)}, u32[]{:S(2)}) copy-start(bf16[2,18,12,512]{3,0,2,1:T(2,128)(2,1)} %param.7) | copy-start | bytes 1327108
  7.2 122.6 %all-gather.5.cloned.1.call-start = ((), (), s32[]{:S(2)}) async-start(), calls=%async_computation | async-start | bytes 6684672 | tf_op jit(solution)/shard_map/all_gather | solution.py:27
  12.1 242.4 %all-gather.7.cloned.1.call-start = ((), (), s32[]{:S(2)}) async-start(), calls=%async_computation.1 | async-start | bytes 6684672 | tf_op jit(solution)/shard_map/all_gather | solution.py:27
  12.2 5.2 %collective-permute-start.2 = (bf16[2,18,6]{1,0,2:T(2,128)(2,1)S(1)}, bf16[2,18,6]{1,0,2:T(2,128)(2,1)S(1)}, u32[]{:S(2)}, u32[]{:S(2)}) collective-permute-start(bf16[2,18,6]{1,0,2:T(2,128)(2,1)S(1)} %get-tuple-element.51), channel_id=1, source_target_pairs={{0,15},{1,0},{2,1},{3,2},{4,3},{5,4},{6,5},{7,6},{8,7},{9,8},{10,9... | collective-permute-start | bytes 1304 | tf_op jit(solution)/shard_map/ppermute | solution.py:16
  17.0 127.0 %copy-start.18 = (bf16[432,512]{1,0:T(8,128)(2,1)}, bf16[432,512]{1,0:T(8,128)(2,1)S(1)}, u32[]{:S(2)}) copy-start(bf16[432,512]{1,0:T(8,128)(2,1)S(1)} %reshape_reshape.34) | copy-start | bytes 1327108
  17.4 3.7 collective-permute-start.3
  140.9 1.5 slice-start
  146.2 3.2 copy-start.27
  168.4 4.5 %copy-start.31 = (f32[3,8,144]{2,1,0:T(8,128)S(1)}, f32[3,8,144]{2,1,0:T(8,128)}, u32[]{:S(2)}) copy-start(f32[3,8,144]{2,1,0:T(8,128)} %get-tuple-element.60) | copy-start | bytes 41476
  169.7 3.2 copy-start.14
  176.9 4.8 %slice-start.1 = ((bf16[16,196608]{1,0:T(8,128)(2,1)}), bf16[16,16384]{1,0:T(8,128)(2,1)S(1)}, s32[]{:S(2)}) async-start(bf16[16,196608]{1,0:T(8,128)(2,1)} %reshape.335), calls=%async_computation.3 | async-start | bytes 1048576 | tf_op jit(solution)/shard_map/slice | solution.py:29
  184.4 3.5 copy-start.6
  189.9 11.1 %copy-start.21 = (bf16[432,512]{1,0:T(8,128)(2,1)S(1)}, bf16[432,512]{1,0:T(8,128)(2,1)}, u32[]{:S(2)}) copy-start(bf16[432,512]{1,0:T(8,128)(2,1)} %reshape.324) | copy-start | bytes 1327108
  189.9 11.7 %copy-start.22 = (bf16[432,512]{1,0:T(8,128)(2,1)S(1)}, bf16[432,512]{1,0:T(8,128)(2,1)}, u32[]{:S(2)}) copy-start(bf16[432,512]{1,0:T(8,128)(2,1)} %reshape.309) | copy-start | bytes 1327108
  201.0 1.8 copy-start.17
  201.0 2.0 copy-start.19
  202.0 8.8 %copy-start.10 = (f32[432,512]{1,0:T(8,128)}, f32[432,512]{1,0:T(8,128)S(1)}, u32[]{:S(2)}) copy-start(f32[432,512]{1,0:T(8,128)S(1)} %get-tuple-element.67) | copy-start | bytes 2654212
  210.8 1.8 copy-start.1
  210.9 3.0 copy-start.2
  213.9 9.6 %copy-start.20 = (bf16[432,512]{1,0:T(8,128)(2,1)S(1)}, bf16[432,512]{1,0:T(8,128)(2,1)}, u32[]{:S(2)}) copy-start(bf16[432,512]{1,0:T(8,128)(2,1)} %copy-done.18) | copy-start | bytes 1327108
  227.2 46.6 %collective-permute-start.6 = (bf16[2,18,6,512]{3,0,2,1:T(2,128)(2,1)}, bf16[2,18,6,512]{3,0,2,1:T(2,128)(2,1)S(1)}, u32[]{:S(2)}, u32[]{:S(2)}) collective-permute-start(bf16[2,18,6,512]{3,0,2,1:T(2,128)(2,1)} %get-tuple-element.37), channel_id=1, source_target_pairs={{0,15},{1,0},{2,1},{3,2},{4,3},{5,4},{6,5},{7,6},{8,7},{9,8},{10,9... | collective-permute-start | bytes 663560 | tf_op jit(solution)/shard_map/ppermute | solution.py:16
  229.3 45.7 %collective-permute-start = (bf16[2,18,6,512]{3,0,2,1:T(2,128)(2,1)}, bf16[2,18,6,512]{3,0,2,1:T(2,128)(2,1)S(1)}, u32[]{:S(2)}, u32[]{:S(2)}) collective-permute-start(bf16[2,18,6,512]{3,0,2,1:T(2,128)(2,1)} %get-tuple-element.39), channel_id=1, source_target_pairs={{0,15},{1,0},{2,1},{3,2},{4,3},{5,4},{6,5},{7,6},{8,7},{9,8},{10,9... | collective-permute-start | bytes 663560 | tf_op jit(solution)/shard_map/ppermute | solution.py:16
  265.1 3.1 slice-start.3
  268.4 3.4 copy-start.7
  273.9 5.0 %collective-permute-start.7 = (bf16[2,3,12,512]{3,0,2,1:T(2,128)(2,1)S(1)}, bf16[2,3,12,512]{3,0,2,1:T(2,128)(2,1)S(1)}, u32[]{:S(2)}, u32[]{:S(2)}) collective-permute-start(bf16[2,3,12,512]{3,0,2,1:T(2,128)(2,1)S(1)} %pad_maximum_fusion.7), channel_id=1, source_target_pairs={{0,240},{16,0},{32,16},{48,32},{64,48},{80,64},{96,80},{112,96},{1... | collective-permute-start | bytes 221192 | tf_op jit(solution)/shard_map/ppermute | solution.py:16
  275.0 2.0 copy-start.28
  275.1 8.4 %collective-permute-start.1 = (bf16[2,3,12,512]{3,0,2,1:T(2,128)(2,1)S(1)}, bf16[2,3,12,512]{3,0,2,1:T(2,128)(2,1)S(1)}, u32[]{:S(2)}, u32[]{:S(2)}) collective-permute-start(bf16[2,3,12,512]{3,0,2,1:T(2,128)(2,1)S(1)} %pad_maximum_fusion.9), channel_id=1, source_target_pairs={{0,240},{16,0},{32,16},{48,32},{64,48},{80,64},{96,80},{112,96},{1... | collective-permute-start | bytes 221192 | tf_op jit(solution)/shard_map/ppermute | solution.py:16
  279.7 2.4 copy-start.24
  284.3 2.4 copy-start.26
  286.7 2.0 copy-start.23
  288.8 4.5 %copy-start.29 = (pred[3,144,144]{1,2,0:T(8,128)(4,1)S(1)}, pred[3,144,144]{1,2,0:T(8,128)(4,1)}, u32[]{:S(2)}) copy-start(pred[3,144,144]{1,2,0:T(8,128)(4,1)} %get-tuple-element.48) | copy-start | bytes 186628
  289.3 8.3 %copy-start.12 = (bf16[3,144,512]{1,2,0:T(8,128)(2,1)}, bf16[3,144,512]{1,2,0:T(8,128)(2,1)S(1)}, u32[]{:S(2)}) copy-start(bf16[3,144,512]{1,2,0:T(8,128)(2,1)S(1)} %copy.114) | copy-start | bytes 1327108
  297.6 3.1 copy-start
  297.6 3.3 copy-start.13
  317.1 3.2 copy-start.15
  320.3 12.8 %copy-start.8 = (f32[432,512]{1,0:T(8,128)}, f32[432,512]{1,0:T(8,128)S(1)}, u32[]{:S(2)}) copy-start(f32[432,512]{1,0:T(8,128)S(1)} %get-tuple-element.79) | copy-start | bytes 2654212
  322.3 1.9 copy-start.16
  322.8 10.3 %copy-start.11 = (f32[432,512]{1,0:T(8,128)}, f32[432,512]{1,0:T(8,128)S(1)}, u32[]{:S(2)}) copy-start(f32[432,512]{1,0:T(8,128)S(1)} %get-tuple-element.81) | copy-start | bytes 2654212
  324.1 9.0 %copy-start.5 = (bf16[2048,512]{1,0:T(8,128)(2,1)S(1)}, bf16[2048,512]{1,0:T(8,128)(2,1)}, u32[]{:S(2)}) copy-start(bf16[2048,512]{1,0:T(8,128)(2,1)} %reshape_reshape.43) | copy-start | bytes 6291460
  333.1 1.8 copy-start.3
  333.1 2.9 copy-start.4
  333.1 2.8 copy-start.25
  348.6 10.8 %collective-permute-start.8 = (bf16[2,18,6,512]{3,0,2,1:T(2,128)(2,1)S(1)}, bf16[2,18,6,512]{3,0,2,1:T(2,128)(2,1)S(1)}, u32[]{:S(2)}, u32[]{:S(2)}) collective-permute-start(bf16[2,18,6,512]{3,0,2,1:T(2,128)(2,1)S(1)} %get-tuple-element.32), channel_id=1, source_target_pairs={{0,1},{1,2},{2,3},{3,4},{4,5},{5,6},{6,7},{7,8},{8,9},{9,10},{10,1... | collective-permute-start | bytes 663560 | tf_op jit(solution)/shard_map/ppermute | solution.py:16
  349.6 12.8 %collective-permute-start.4 = (bf16[2,18,6,512]{3,0,2,1:T(2,128)(2,1)S(1)}, bf16[2,18,6,512]{3,0,2,1:T(2,128)(2,1)S(1)}, u32[]{:S(2)}, u32[]{:S(2)}) collective-permute-start(bf16[2,18,6,512]{3,0,2,1:T(2,128)(2,1)S(1)} %get-tuple-element.34), channel_id=1, source_target_pairs={{0,1},{1,2},{2,3},{3,4},{4,5},{5,6},{6,7},{7,8},{8,9},{9,10},{10,1... | collective-permute-start | bytes 663560 | tf_op jit(solution)/shard_map/ppermute | solution.py:16
  359.6 6.0 %collective-permute-start.9 = (bf16[2,3,12,512]{3,0,2,1:T(2,128)(2,1)S(1)}, bf16[2,3,12,512]{3,0,2,1:T(2,128)(2,1)S(1)}, u32[]{:S(2)}, u32[]{:S(2)}) collective-permute-start(bf16[2,3,12,512]{3,0,2,1:T(2,128)(2,1)S(1)} %pad_maximum_fusion.6), channel_id=1, source_target_pairs={{0,16},{16,32},{32,48},{48,64},{64,80},{80,96},{96,112},{112,128},... | collective-permute-start | bytes 221192 | tf_op jit(solution)/shard_map/ppermute | solution.py:16
  362.5 6.0 %collective-permute-start.5 = (bf16[2,3,12,512]{3,0,2,1:T(2,128)(2,1)S(1)}, bf16[2,3,12,512]{3,0,2,1:T(2,128)(2,1)S(1)}, u32[]{:S(2)}, u32[]{:S(2)}) collective-permute-start(bf16[2,3,12,512]{3,0,2,1:T(2,128)(2,1)S(1)} %pad_maximum_fusion.8), channel_id=1, source_target_pairs={{0,16},{16,32},{32,48},{48,64},{64,80},{80,96},{96,112},{112,128},... | collective-permute-start | bytes 221192 | tf_op jit(solution)/shard_map/ppermute | solution.py:16
  (2 other events, 2.4 us)
Sparse Core Ops, SparseCore 0:
  12.2 117.5 all-gather.4
  132.3 122.0 all-gather.6
where the time goes:
time: 381 us; the launch traced here: 377 us
  waiting for transfers between devices  143 us (38%)
  local copies, waits for them, and re-layouts  91.9 us (24%)
  matrix products  86.3 us (23%)
  other arithmetic  23.5 us (6%)
  starting transfers between devices  16.6 us (4%)
  between operations  15.2 us (4%)
    all_gather x2, waiting for transfers between devices, gather_packed(): lines, at, finished = (lax.all_gather(flat, axis), 0, [])  130 us
    dot_general x8, matrix products, direct(): jnp.dot(streams[0], complete, preferred_element_type=jnp.float32)  24.8 us
    another operation x8, local copies, waits for them, and re-layouts, joined_along(): pieces.reshape(*dims[:dim], dims[dim] * dims[dim + 1], *dims[dim + 2:])  22.2 us
    dot_general x6, matrix products, direct(): jnp.dot(streams[1], complete, preferred_element_type=jnp.float32)  20.1 us
    ppermute x10, starting transfers between devices, from_behind(): lax.ppermute(x, axis, [(i, (i + by) % length) for i in range(length)])  16.6 us
    dot_general x4, matrix products, window_attention(): jnp.einsum('wqhe,wkhe->whqk', queries, keys_all, preferred_element_type=j...  16.2 us
    dot_general x6, matrix products, window_attention(): jnp.einsum('whqk,wkhe->wqhe', probs, values_all, preferred_element_type=j...  15.6 us
    ppermute x10, waiting for transfers between devices, from_behind(): lax.ppermute(x, axis, [(i, (i + by) % length) for i in range(length)])  13.8 us
  transfers between devices with their start and end apart: 12, of which 8 were waited for; matrix products, arithmetic and copies ran while one was open for 33% of the time, Pallas kernels for 0%

commit v1 on v0

v1 whole, which is shorter than its diff:
```python
import functools

import jax
import jax.numpy as jnp
import numpy as np
from jax import lax
from jax.experimental import pallas as pl
from jax.experimental.pallas import tpu as pltpu
from jax.sharding import PartitionSpec as P

D = 512
FF = 2048
T = 144
WINDOWS = 3
UNIT = 36
SLOT = 48
NORM_EPSILON = 1e-5
MESH = pl.DeviceIdType.MESH
BF = jnp.bfloat16
F32 = jnp.float32


def unit_order():
    order = np.zeros((T, 4 * SLOT), np.float32)
    for i in range(T):
        row, col, level = i // 24, i % 24 // 2, i % 2
        unit = (col // 6) * 2 + row // 3
        order[i, unit * SLOT + (row % 3) * 12 + (col % 6) * 2 + level] = 1
    return order


def dot(a, b):
    return jnp.dot(a, b, preferred_element_type=F32)


def dot_nt(a, b):
    return lax.dot_general(a, b, (((1,), (1,)), ((), ())), preferred_element_type=F32)


def iota(shape, dim):
    return lax.broadcasted_iota(jnp.int32, shape, dim)


def norm_pair(y, dy):
    y = y - jnp.mean(y, -1, keepdims=True)
    scale = lax.rsqrt(jnp.mean(y * y, -1, keepdims=True) + NORM_EPSILON)
    n = y * scale
    dy = dy - jnp.mean(dy, -1, keepdims=True)
    return n, scale * (dy - n * jnp.mean(n * dy, -1, keepdims=True))


def key_caps(mask_rows, edge):
    query, key = iota((T, T), 0), iota((T, T), 1)
    pick = (iota((8, 128), 1) == 0).astype(BF)
    usable = dot_nt(pick, mask_rows.astype(BF))[0:1]
    apart = ((query >= T // 2) != (key >= T // 2)).astype(jnp.int32) * edge
    allowed = ((usable > 0.5) & (apart == 0)) | (query == key)
    return jnp.where(allowed, 3e38, -1e9).astype(F32)


def project_qkv(xx, wa, pk):
    for part in range(3):
        cols = slice(part * D, (part + 1) * D)
        out = dot(xx, wa[:, cols]).astype(BF)
        pk[:, cols] = out * BF(0.125) if part == 0 else out


def head_pair(p, pk, caps, att):
    at = lambda part: pl.ds(pl.multiple_of(part * D + p * 128, 128), 128)
    first = iota((T, 128), 1) < 64
    zero = jnp.zeros((T, 128), BF)
    q, dq = pk[:T, at(0)], pk[T:, at(0)]
    keys = jnp.concatenate([pk[:T, at(1)], pk[T:, at(1)]], 1)
    values = jnp.concatenate([pk[:T, at(2)], pk[T:, at(2)]], 1)
    outs = []
    for keep in (first, ~first):
        qh, dqh = jnp.where(keep, q, zero), jnp.where(keep, dq, zero)
        left = jnp.concatenate(
            [jnp.concatenate([qh, zero], 1), jnp.concatenate([dqh, qh], 1)], 0
        )
        both = dot_nt(left, keys)
        s, ds = jnp.minimum(both[:T], caps[...]), both[T:]
        e = jnp.exp(s - jnp.max(s, -1, keepdims=True))
        prob = e * (1.0 / jnp.sum(e, -1, keepdims=True))
        dprob = prob * (ds - jnp.sum(prob * ds, -1, keepdims=True))
        probs = jnp.concatenate([prob.astype(BF), dprob.astype(BF)], 0)
        mixed = dot(probs, values)
        outs.append((mixed[:T, :128], mixed[T:, :128] + mixed[:T, 128:]))
    att[:T, at(0)] = jnp.where(first, outs[0][0], outs[1][0]).astype(BF)
    att[T:, at(0)] = jnp.where(first, outs[0][1], outs[1][1]).astype(BF)


def project_out(xx, att, wa, hid):
    out = dot(att[...], wa[:, 3 * D :])
    n, dn = norm_pair(out[:T], out[T:])
    hid[:T] = xx[:T].astype(F32) + n
    hid[T:] = xx[T:].astype(F32) + dn


def mlp_chunk(j, hb, wb, wc, acc):
    cols = pl.ds(pl.multiple_of(j * D, D), D)
    up = dot(hb[...], wb[:, cols])
    u, du = up[:T], up[T:]
    cdf = 0.5 + 0.5 * lax.erf(u * np.float32(0.5**0.5))
    pdf = jnp.exp(u * u * -0.5) * np.float32((2 * np.pi) ** -0.5)
    act = jnp.concatenate([(u * cdf).astype(BF), (du * (cdf + u * pdf)).astype(BF)], 0)
    acc[...] += dot(act, wc[cols, :])


def kernel(
    x_ref, code_ref, to_tokens, to_units, wqkv, wout, wup, wdown, out0, out1,
    wa, wb, wc, units, staged, results, returned, mask_units, mask_staged,
    xx, hid, hb, acc, pk, att, caps,
    load_sem, ring_send, ring_recv, mask_send, mask_recv,
    ahead_send, ahead_recv, back_send, back_recv,
):
    lat, lon = lax.axis_index("lat"), lax.axis_index("lon")
    n_lat, n_lon = 16, 16
    core, z = lax.rem(lat, 2), lon // 2
    step_lat = lambda by: lax.rem(lat + by + n_lat, n_lat)
    step_lon = lambda by: lax.rem(lon + by + n_lon, n_lon)
    side_lat = lat + 2 - 4 * lax.rem(lat // 2, 2)
    side_lon = lon + 1 - 2 * lax.rem(lon, 2)
    twin = (lat + 1 - 2 * core, lon)
    across = (side_lat, side_lon)
    z_up, z_down = (lat, step_lon(2)), (lat, step_lon(-2))
    west, east = (lat, step_lon(-1)), (lat, step_lon(1))
    north, south = (step_lat(-1), lon), (step_lat(1), lon)
    north_west, south_east = (step_lat(-1), step_lon(-1)), (step_lat(1), step_lon(1))

    loads = []
    for b in range(2):
        rows = pl.ds(pl.multiple_of(lon * 32, 32), 32)
        deep = pl.ds(pl.multiple_of(lon * 128, 128), 128)
        loads += [
            pltpu.make_async_copy(wqkv.at[b], wa.at[b, rows, pl.ds(0, 3 * D)], load_sem.at[4 * b]),
            pltpu.make_async_copy(wout.at[b], wa.at[b, rows, pl.ds(3 * D, D)], load_sem.at[4 * b + 1]),
            pltpu.make_async_copy(wup.at[b], wb.at[b, rows, :], load_sem.at[4 * b + 2]),
            pltpu.make_async_copy(wdown.at[b], wc.at[b, deep, :], load_sem.at[4 * b + 3]),
        ]
    for load in loads:
        load.start()

    barrier = pltpu.get_barrier_semaphore()
    friends = (twin, across, z_up, z_down, west, east, north, south, north_west, south_east)
    for friend in friends:
        pl.semaphore_signal(barrier, inc=1, device_id=friend, device_id_type=MESH)

    for w in range(WINDOWS):
        mask = (code_ref[w * T : (w + 1) * T] >= D).astype(BF)
        spread = dot(to_units[...], jnp.broadcast_to(mask, (T, 128))).astype(BF)
        spread = spread.reshape(2, 2, SLOT, 128)
        mask_staged[2 * w : 2 * w + 2] = spread[0]
        mask_units[0, 2 * w : 2 * w + 2] = spread[1]

    pl.semaphore_wait(barrier, len(friends))

    full = [(ref.at[b], unit, half) for b in range(2) for ref, unit, half in ((wa, 64, 1024), (wb, 64, 1024), (wc, 256, 256))]

    def copy(k, slot, rows, cols, device):
        place = full[k][0].at[rows, cols]
        return pltpu.make_async_remote_copy(
            src_ref=place, dst_ref=place, send_sem=ring_send.at[k, slot], recv_sem=ring_recv.at[k, slot],
            device_id=device, device_id_type=MESH,
        )

    def pieces(k):
        _, unit, half = full[k]
        mine = pl.ds(pl.multiple_of(core * half, half), half)
        other = pl.ds(pl.multiple_of((1 - core) * half, half), half)
        low = pl.ds(pl.multiple_of(core * half, half // 2), half // 2)
        high = pl.ds(pl.multiple_of(core * half + half // 2, half // 2), half // 2)
        shard = lambda o: pl.ds(pl.multiple_of(o * (unit // 2), unit // 2), unit // 2)
        block = lambda by: pl.ds(pl.multiple_of(lax.rem(z + by + 8, 8) * unit, unit), unit)
        table = {"x": (0, shard(lon), shard(side_lon), mine, mine, across)}
        table["sx"] = (1, shard(side_lon), shard(side_lon), mine, other, twin)
        for t in (1, 2, 3, 4):
            table[f"u{t}"] = (2 * t, block(1 - t), block(-t), low if t == 4 else mine, low if t == 4 else mine, z_up)
            table[f"d{t}"] = (2 * t + 1, block(t - 1), block(t), high if t == 4 else mine, high if t == 4 else mine, z_down)
            table[f"su{t}"] = (8 + 2 * t, block(-t), block(-t), mine, other, twin)
            if t < 4:
                table[f"sd{t}"] = (9 + 2 * t, block(t), block(t), mine, other, twin)
        return table

    tables = [pieces(k) for k in range(6)]

    def send(k, *names):
        for name in names:
            slot, rows, _, cols, _, device = tables[k][name]
            copy(k, slot, rows, cols, device).start()

    def arrive(k, *names):
        for name in names:
            slot, _, rows, _, cols, device = tables[k][name]
            copy(k, slot, rows, cols, device).wait_recv()

    def ring(k, step):
        if step == 0:
            for load in loads[4 * (k // 3) :][((0, 1), (2,), (3,))[k % 3][0] : ((0, 1), (2,), (3,))[k % 3][-1] + 1]:
                load.wait()
            send(k, "x")
        elif step == 1:
            arrive(k, "x")
            send(k, "u1", "d1", "sx")
        elif step in (2, 3, 4):
            t = step - 1
            arrive(k, f"u{t}")
            send(k, f"u{step}")
            arrive(k, f"d{t}")
            send(k, f"d{step}")
            send(k, f"su{t}", f"sd{t}")
        elif step == 5:
            arrive(k, "u4", "d4")
            send(k, "su4")
        else:
            arrive(k, "sx", "su1", "sd1", "su2", "sd2", "su3", "sd3", "su4")

    def ring_end(k):
        for slot, rows, _, cols, _, device in tables[k].values():
            copy(k, slot, rows, cols, device).wait_send()

    def remote(src, dst, sems, slot, device):
        return pltpu.make_async_remote_copy(
            src_ref=src, dst_ref=dst, send_sem=sems[0].at[slot], recv_sem=sems[1].at[slot],
            device_id=device, device_id_type=MESH,
        )

    masks_out = [
        remote(mask_staged.at[pl.ds(1, 5)], mask_units.at[1, pl.ds(1, 5)], (mask_send, mask_recv), 0, west),
        remote(mask_staged.at[pl.ds(0, 1)], mask_units.at[1, pl.ds(6, 1)], (mask_send, mask_recv), 1, north_west),
        remote(mask_units.at[0, pl.ds(0, 1)], mask_units.at[0, pl.ds(6, 1)], (mask_send, mask_recv), 2, north),
    ]
    ahead = (ahead_send, ahead_recv)
    ahead_out = [
        [
            remote(staged.at[pl.ds(1, 1)], units.at[1, pl.ds(1, 1)], ahead, 0, west),
            remote(staged.at[pl.ds(0, 1)], units.at[1, pl.ds(6, 1)], ahead, 3, north_west),
            remote(units.at[0, pl.ds(0, 1)], units.at[0, pl.ds(6, 1)], ahead, 4, north),
        ],
        [remote(staged.at[pl.ds(2, 2)], units.at[1, pl.ds(2, 2)], ahead, 1, west)],
        [remote(staged.at[pl.ds(4, 2)], units.at[1, pl.ds(4, 2)], ahead, 2, west)],
    ]
    back = (back_send, back_recv)
    back_out = [
        [remote(returned.at[pl.ds(1, 2)], results.at[0, pl.ds(1, 2)], back, 0, east)],
        [remote(returned.at[pl.ds(3, 2)], results.at[0, pl.ds(3, 2)], back, 1, east)],
        [
            remote(returned.at[pl.ds(5, 1)], results.at[0, pl.ds(5, 1)], back, 2, east),
            remote(returned.at[pl.ds(6, 1)], results.at[0, pl.ds(0, 1)], back, 3, south_east),
            remote(results.at[1, pl.ds(6, 1)], results.at[1, pl.ds(0, 1)], back, 4, south),
        ],
    ]

    for k in range(6):
        ring(k, 0)
        if k == 0:
            for c in masks_out:
                c.start()
    for k, step in PROLOGUE:
        ring(k, step)

    def at_points(point, table):
        for n, events in table.items():

            @pl.when(point == n)
            def _():
                for k, step in events:
                    ring(k, step)

    edge_row = (lat == n_lat - 1).astype(jnp.int32)

    for b in range(2):
        edge = b == 1

        def phase_attention(w, carry):
            if b == 0:
                rows = pl.ds(pl.multiple_of(w * T, 16), T)
                code = code_ref[rows]
                hot = (iota((T, D), 1) == lax.rem(code, D)).astype(BF)
                xx[w, :T] = x_ref[rows]
                xx[w, T:] = hot
                caps[...] = key_caps(jnp.broadcast_to((code >= D).astype(F32), (T, 128)), 0)
            else:

                @pl.when(w == 0)
                def _():
                    for c in (*masks_out, ahead_out[0][0], *ahead_out[1]):
                        c.wait_recv()

                @pl.when(w == 1)
                def _():
                    for c in ahead_out[2]:
                        c.wait_recv()

                @pl.when(w == 2)
                def _():
                    for c in ahead_out[0][1:]:
                        c.wait_recv()

                slots = pl.ds(2 * w + 1, 2)
                for s in range(2):
                    got = units[:, slots, s].reshape(4 * SLOT, D)
                    xx[w, s * T : (s + 1) * T] = dot(to_tokens[...], got).astype(BF)
                masks = mask_units[:, slots].reshape(4 * SLOT, 128)
                last = (w == WINDOWS - 1).astype(jnp.int32)
                caps[...] = key_caps(dot(to_tokens[...], masks), edge_row * last)
            project_qkv(xx[w], wa.at[b], pk)

            def pair(p, carry):
                head_pair(p, pk, caps, att)
                at_points(w * 4 + p, ATTENTION_POINTS[b])
                return carry

            lax.fori_loop(0, 4, pair, 0)
            project_out(xx.at[w], att, wa.at[b], hid.at[w])
            return carry

        lax.fori_loop(0, WINDOWS, phase_attention, 0)
        for k, step in BETWEEN[b]:
            ring(k, step)

        def phase_mlp(w, carry):
            hb[...] = hid[w].astype(BF)
            acc[...] = jnp.zeros_like(acc)

            def chunk(j, carry):
                mlp_chunk(j, hb, wb.at[b], wc.at[b], acc)
                at_points(w * 4 + j, MLP_POINTS[b])
                return carry

            lax.fori_loop(0, 4, chunk, 0)
            n, dn = norm_pair(acc[:T], acc[T:])
            for s, grown in ((0, n), (1, dn)):
                final = (hid[w, s * T : (s + 1) * T] + grown).astype(BF)
                spread = dot(to_units[...], final).astype(BF).reshape(2, 2, SLOT, D)
                if b == 0:
                    staged[pl.ds(2 * w, 2), s] = spread[0]
                    units[0, pl.ds(2 * w, 2), s] = spread[1]
                else:
                    results[1, pl.ds(2 * w + 1, 2), s] = spread[0]
                    returned[pl.ds(2 * w + 1, 2), s] = spread[1]
            for i in range(WINDOWS):

                @pl.when(w == i)
                def _():
                    for c in (ahead_out, back_out)[b][i]:
                        c.start()

            return carry

        lax.fori_loop(0, WINDOWS, phase_mlp, 0)
        for k, step in AFTER[b]:
            ring(k, step)

    for w, waits in ((1, (*back_out[0], *back_out[1])), (2, back_out[2][:1]), (0, back_out[2][1:])):
        for c in waits:
            c.wait_recv()
        for s, out in ((0, out0), (1, out1)):
            got = results[:, 2 * w : 2 * w + 2, s].reshape(4 * SLOT, D)
            out[w * T : (w + 1) * T] = dot(to_tokens[...], got).astype(BF)
    for k in range(6):
        ring_end(k)
    for c in (*masks_out, *sum(ahead_out, []), *sum(back_out, [])):
        c.wait_send()


PROLOGUE = (
    (0, 1), (0, 2), (1, 1), (0, 3), (0, 4), (1, 2), (0, 5), (0, 6),
)
ATTENTION_POINTS = (
    {0: [(2, 1)], 1: [(1, 3)], 2: [(2, 2)], 3: [(1, 4)], 4: [(2, 3)], 5: [(1, 5)], 6: [(2, 4)], 8: [(2, 5)], 9: [(3, 1)], 11: [(3, 2)]},
    {0: [(4, 1)], 1: [(4, 2)], 2: [(5, 1)], 3: [(4, 3)], 4: [(5, 2)], 5: [(4, 4)], 6: [(5, 3)], 7: [(4, 5)], 8: [(5, 4)], 10: [(5, 5)]},
)
BETWEEN = (((1, 6), (2, 6)), ((4, 6), (5, 6)))
MLP_POINTS = (
    {1: [(3, 3)], 3: [(3, 4)], 6: [(3, 5)]},
    {},
)
AFTER = (((3, 6),), ())


def on_device(fields, tangent_pick, key_mask, w_qkv, w_out, w_up, w_down):
    levels, rows, cols, _ = fields.shape
    tokens = levels * rows * cols
    x = jnp.transpose(fields, (1, 2, 0, 3)).reshape(tokens, D)
    code = jnp.transpose(tangent_pick + D * key_mask, (1, 2, 0)).reshape(tokens, 1)
    order = unit_order()
    to_tokens = jnp.asarray(order, BF)
    to_units = jnp.asarray(order.T, BF)
    vmem, hbm = pl.BlockSpec(memory_space=pltpu.VMEM), pl.BlockSpec(memory_space=pl.ANY)
    dma = pltpu.SemaphoreType.DMA
    outs = pl.pallas_call(
        kernel,
        out_shape=[jax.ShapeDtypeStruct((tokens, D), BF)] * 2,
        in_specs=[vmem] * 4 + [hbm] * 4,
        out_specs=[vmem] * 2,
        scratch_shapes=[
            pltpu.VMEM((2, D, 4 * D), BF),
            pltpu.VMEM((2, D, FF), BF),
            pltpu.VMEM((2, FF, D), BF),
            pltpu.VMEM((2, 7, 2, SLOT, D), BF),
            pltpu.VMEM((6, 2, SLOT, D), BF),
            pltpu.VMEM((2, 7, 2, SLOT, D), BF),
            pltpu.VMEM((7, 2, SLOT, D), BF),
            pltpu.VMEM((2, 7, SLOT, 128), BF),
            pltpu.VMEM((6, SLOT, 128), BF),
            pltpu.VMEM((WINDOWS, 2 * T, D), BF),
            pltpu.VMEM((WINDOWS, 2 * T, D), F32),
            pltpu.VMEM((2 * T, D), BF),
            pltpu.VMEM((2 * T, D), F32),
            pltpu.VMEM((2 * T, 3 * D), BF),
            pltpu.VMEM((2 * T, D), BF),
            pltpu.VMEM((T, T), F32),
            dma((8,)),
            dma((6, 17)),
            dma((6, 17)),
            dma((3,)),
            dma((3,)),
            dma((5,)),
            dma((5,)),
            dma((5,)),
            dma((5,)),
        ],
        compiler_params=pltpu.CompilerParams(
            collective_id=0, has_side_effects=True, vmem_limit_bytes=52 * 1024 * 1024
        ),
        name="swin",
    )(x, code, to_tokens, to_units, w_qkv, w_out, w_up, w_down)
    return tuple(
        jnp.transpose(o.reshape(rows, cols, levels, D), (2, 0, 1, 3)) for o in outs
    )


def solution(mesh):
    weight = P(None, "lon", None)
    grid = P(None, "lat", "lon")
    field = P(None, "lat", "lon", None)
    return jax.shard_map(
        on_device,
        mesh=mesh,
        in_specs=(field, grid, grid, weight, weight, weight, weight),
        out_specs=(field, field),
        check_vma=False,
    )
```

time: 381 us -> 144 us (0.38)
  the two profiles are of different devices: /device:TPU:64 before, /device:TPU:25 now
where the time goes in v1:
time: 144 us
  Pallas kernels  139 us (97%)
  local copies, waits for them, and re-layouts  3.32 us (2%)
    pallas_call x1, Pallas kernels, on_device(): pl.pallas_call(kernel, out_shape=[jax.ShapeDtypeStruct((tokens, D), BF)]...  139 us

profile of v1, /device:TPU:25, one launch (start us, length us, event | category | flops | bytes accessed | tf_op | source)
XLA Modules:
  0.0 144.2 jit_solution(14740272235527773176)
XLA Ops:
  0.6 0.0 copy-start.6
  0.6 0.8 add_bitcast_fusion
  1.4 0.2 copy.12
  1.6 0.0 copy-start.4
  1.6 0.1 reshape.20.code_ref
  1.7 0.0 copy-done.6
  1.7 0.0 copy-start
  1.7 0.0 copy-start.1
  1.8 0.0 copy-start.2
  1.8 0.0 copy-start.3
  1.8 0.0 copy-start.5
  1.8 0.9 reshape.16.x_ref
  2.7 0.0 copy-done.4
  2.7 0.0 copy-done
  2.7 0.0 copy-done.1
  2.8 0.1 copy-done.2
  2.8 0.0 copy-done.3
  2.9 0.0 copy-done.5
  2.9 139.3 %swin.1 = (bf16[432,512]{1,0:T(8,128)(2,1)S(1)}, bf16[432,512]{1,0:T(8,128)(2,1)}) custom-call(bf16[432,512]{1,0:T(8,128)(2,1)} %reshape.16.x_ref, s32[432,1]{1,0:T(8,128)S(1)} %reshape.20.code_ref, bf16[144,192]{1,0:T(8,128)(2,1)S(1)} %copy-done.4, bf16[192,144]{1,0:T(8,128)(2,1)S(1)} %copy-done.3, bf16[2,32,1536]{2,1,0:T(8,128)(2,1)S(1)} %copy-done.2, ...), custom_call_target="tpu_custom_call" | custom-call | tf_op jit(solution)/shard_map/swin/pallas_call | solution.py:392
  142.2 0.0 copy-start.7
  142.2 0.9 reshape.18
  143.1 0.1 copy-done.7
  143.2 0.9 reshape.19
Async XLA Ops:
  0.6 1.1 copy-start.6
  1.6 1.1 copy-start.4
  1.7 1.0 copy-start
  1.7 1.0 copy-start.1
  1.8 1.1 copy-start.2
  1.8 1.1 copy-start.3
  1.8 1.1 copy-start.5
  142.2 1.0 copy-start.7

commit v2 on v1

v2 whole, which is shorter than its diff:
```python
import functools

import jax
import jax.numpy as jnp
import numpy as np
from jax import lax
from jax.experimental import pallas as pl
from jax.experimental.pallas import tpu as pltpu
from jax.sharding import PartitionSpec as P

D = 512
FF = 2048
T = 144
WINDOWS = 3
UNIT = 36
SLOT = 48
NORM_EPSILON = 1e-5
MESH = pl.DeviceIdType.MESH
BF = jnp.bfloat16
F32 = jnp.float32


def unit_order():
    order = np.zeros((T, 4 * SLOT), np.float32)
    for i in range(T):
        row, col, level = i // 24, i % 24 // 2, i % 2
        unit = (col // 6) * 2 + row // 3
        order[i, unit * SLOT + (row % 3) * 12 + (col % 6) * 2 + level] = 1
    return order


def dot(a, b):
    return jnp.dot(a, b, preferred_element_type=F32)


def dot_nt(a, b):
    return lax.dot_general(a, b, (((1,), (1,)), ((), ())), preferred_element_type=F32)


def dot_tn(a, b):
    return lax.dot_general(a, b, (((0,), (0,)), ((), ())), preferred_element_type=F32)


def iota(shape, dim):
    return lax.broadcasted_iota(jnp.int32, shape, dim)


def norm_pair(y, dy):
    y = y - jnp.mean(y, -1, keepdims=True)
    scale = lax.rsqrt(jnp.mean(y * y, -1, keepdims=True) + NORM_EPSILON)
    n = y * scale
    dy = dy - jnp.mean(dy, -1, keepdims=True)
    return n, scale * (dy - n * jnp.mean(n * dy, -1, keepdims=True))


def key_caps(usable, edge):
    key, query = iota((T, 2 * T), 0), iota((T, 2 * T), 1)
    query = jnp.where(query >= T, query - T, query)
    apart = ((query >= T // 2) != (key >= T // 2)).astype(jnp.int32) * edge
    allowed = ((usable > 0.5) & (apart == 0)) | (query == key)
    return jnp.where(allowed, 3e38, -1e9).astype(F32)


def project_qkv(xx, wa, pk):
    for part in range(3):
        cols = slice(part * 256, (part + 1) * 256)
        out = dot(xx, wa[:, cols]).astype(BF)
        pk[:, cols] = out * BF(0.125) if part == 0 else out


def head_pair(p, pk, caps, att):
    at = lambda part: pl.ds(pl.multiple_of(part * 256 + p * 128, 128), 128)
    first = iota((T, 128), 1) < 64
    zero = jnp.zeros((T, 128), BF)
    split = lambda a: jnp.concatenate([jnp.where(first, a, zero), jnp.where(first, zero, a)], 0)
    q, dq = split(pk[:T, at(0)]), split(pk[T:, at(0)])
    k, v = pk[:T, at(1)], pk[:T, at(2)]
    keys = jnp.concatenate([k, pk[T:, at(1)]], 1)
    values = jnp.concatenate([v, pk[T:, at(2)]], 1)
    s = jnp.minimum(dot_nt(k, q), caps[...])
    ds = dot_nt(keys, jnp.concatenate([dq, q], 1))
    e = jnp.exp(s - jnp.max(s, 0, keepdims=True))
    prob = e * (1.0 / jnp.sum(e, 0, keepdims=True))
    dprob = prob * (ds - jnp.sum(prob * ds, 0, keepdims=True))
    mixed = dot_tn(prob.astype(BF), values)
    dmixed = dot_tn(dprob.astype(BF), v) + mixed[:, 128:]
    att[:T, at(0)] = jnp.where(first, mixed[:T, :128], mixed[T:, :128]).astype(BF)
    att[T:, at(0)] = jnp.where(first, dmixed[:T], dmixed[T:]).astype(BF)


def project_out(xx, att, wa, hid):
    out = jnp.concatenate([dot(jnp.concatenate([att[0], att[1]], 1), wa[s, :, 768:]) for s in range(2)], 1)
    n, dn = norm_pair(out[:T], out[T:])
    hid[:T] = xx[:T].astype(F32) + n
    hid[T:] = xx[T:].astype(F32) + dn


def up_chunk(j, hb, wb, act):
    cols = pl.ds(pl.multiple_of(j * D, D), D)
    up = dot(hb[...], wb[:, cols])
    u, du = up[:T], up[T:]
    cdf = 0.5 + 0.5 * lax.erf(u * np.float32(0.5**0.5))
    pdf = jnp.exp(u * u * -0.5) * np.float32((2 * np.pi) ** -0.5)
    act[:T, cols] = (u * cdf).astype(BF)
    act[T:, cols] = (du * (cdf + u * pdf)).astype(BF)


def kernel(
    x_ref, code_ref, to_tokens, to_units, wqkv, wout, wup, wdown, out0, out1,
    own_a, own_b, own_c, wa, wb, wc, units, staged, results, returned, mask_units, mask_staged,
    xx, hid, hb, act, pk, att, caps,
    load_sem, keep_sem, ring_send, ring_recv, mask_send, mask_recv,
    ahead_send, ahead_recv, back_send, back_recv,
):
    lat, lon = lax.axis_index("lat"), lax.axis_index("lon")
    n_lat, n_lon = 16, 16
    core, x_lo, y, x_hi, z = lax.rem(lat, 2), lax.rem(lat // 2, 2), lat // 4, lax.rem(lon, 2), lon // 2
    color = lax.rem(2 * x_lo + y, 4)
    step_lat = lambda by: lax.rem(lat + by + n_lat, n_lat)
    step_lon = lambda by: lax.rem(lon + by + n_lon, n_lon)
    side_lat = lat + 2 - 4 * x_lo
    side_lon = lon + 1 - 2 * x_hi
    twin = (lat + 1 - 2 * core, lon)
    beside = (side_lat, lon)
    y_up, y_down = (step_lat(4), lon), (step_lat(-4), lon)
    peers = [(lat, step_lon(2 * t)) for t in range(1, 8)]
    side_peers = [(side_lat, lax.rem(side_lon + 2 * t, n_lon)) for t in range(8)]
    west, east = (lat, step_lon(-1)), (lat, step_lon(1))
    north, south = (step_lat(-1), lon), (step_lat(1), lon)
    north_west, south_east = (step_lat(-1), step_lon(-1)), (step_lat(1), step_lon(1))

    loads = []
    for b in range(2):
        for s in range(2):
            loads.append([])
            for part in range(4):
                src = wqkv.at[b, :, pl.ds(part * D + s * 256, 256)] if part < 3 else wout.at[b, :, pl.ds(s * 256, 256)]
                loads[-1].append((src, own_a.at[b, s, :, pl.ds(part * 256, 256)], 10 * b + 4 * s + part))
        loads.append([(wup.at[b], own_b.at[b], 10 * b + 8)])
        loads.append([(wdown.at[b], own_c.at[b, 0], 10 * b + 9)])
    loads = [[pltpu.make_async_copy(src, dst, load_sem.at[i]) for src, dst, i in group] for group in loads]
    for group in loads:
        for load in group:
            load.start()

    barrier = pltpu.get_barrier_semaphore()
    friends = (*peers, *side_peers, twin, beside, y_up, y_down, west, east, north, south, north_west, south_east)
    for friend in friends:
        pl.semaphore_signal(barrier, inc=1, device_id=friend, device_id_type=MESH)

    for w in range(WINDOWS):
        mask = (code_ref[w * T : (w + 1) * T] >= D).astype(BF)
        spread = dot(to_units[...], jnp.broadcast_to(mask, (T, 128))).astype(BF)
        spread = spread.reshape(2, 2, SLOT, 128)
        mask_staged[2 * w : 2 * w + 2] = spread[0]
        mask_units[0, 2 * w : 2 * w + 2] = spread[1]

    pl.semaphore_wait(barrier, len(friends))

    def block(k, of_core, of_color, part):
        b, kind = k // 4, k % 4
        if kind == 3:
            rows = {"all": pl.ds(0, 16), "own": pl.ds(lon, 1), "rest": pl.ds(0, 15)}[part]
            depth = pl.ds(pl.multiple_of(of_core * 64, 64), 64)
            return wc.at[b, rows, depth, pl.ds(pl.multiple_of(of_color * 128, 128), 128)]
        rows = {
            "all": pl.ds(0, 512), "own": pl.ds(pl.multiple_of(lon * 32, 32), 32), "rest": pl.ds(0, 480),
        }[part]
        width = 256 if kind == 2 else 128
        cols = pl.ds(pl.multiple_of((of_core * 4 + of_color) * width, width), width)
        return wb.at[b, rows, cols] if kind == 2 else wa.at[b, kind, rows, cols]

    def own(k, of_color):
        b, kind = k // 4, k % 4
        if kind == 3:
            depth = pl.ds(pl.multiple_of(core * 64, 64), 64)
            return own_c.at[b, :, depth, pl.ds(pl.multiple_of(of_color * 128, 128), 128)]
        width = 256 if kind == 2 else 128
        cols = pl.ds(pl.multiple_of((core * 4 + of_color) * width, width), width)
        return own_b.at[b, :, cols] if kind == 2 else own_a.at[b, kind, :, cols]

    def keep(k):
        return pltpu.make_async_copy(own(k, color), block(k, core, color, "own"), keep_sem.at[k])

    def copy(k, slot, place, device, source=None):
        return pltpu.make_async_remote_copy(
            src_ref=place if source is None else source, dst_ref=place, send_sem=ring_send.at[k, slot], recv_sem=ring_recv.at[k, slot],
            device_id=device, device_id_type=MESH,
        )

    other = 1 - core
    shades = [lax.rem(color + t, 4) for t in range(4)]

    def inward(k):
        mine = lambda part: block(k, core, color, part)
        return (
            (1, mine("all"), block(k, core, shades[3], "all"), y_up),
            (2, mine("all"), block(k, core, shades[1], "all"), y_down),
            (3, mine("all"), block(k, core, shades[2], "all"), beside),
        )

    def paired(k):
        return tuple((4 + t, block(k, core, shades[t], "all"), block(k, other, shades[t], "all"), twin) for t in range(4))

    def ring(k, step):
        if step == 1:
            for load in loads[k]:
                load.wait()
            keep(k).start()
            for t in (1, 7, 2, 6, 3, 5, 4):
                copy(k, 0, block(k, core, color, "own"), peers[t - 1], own(k, color)).start()
                if t == 1:
                    copy(k, 0, block(k, core, shades[2], "own"), side_peers[0], own(k, shades[2])).start()
                copy(k, 0, block(k, core, shades[2], "own"), side_peers[t], own(k, shades[2])).start()
        elif step == 2:
            keep(k).wait()
            copy(k, 0, block(k, core, color, "rest"), twin).wait_recv()
            for slot, mine, _, device in inward(k):
                copy(k, slot, mine, device).start()
            slot, mine, _, device = paired(k)[0]
            copy(k, slot, mine, device).start()
        elif step == 3:
            for slot, _, theirs, device in inward(k):
                copy(k, slot, theirs, device).wait_recv()
            for slot, mine, _, device in paired(k)[1:]:
                copy(k, slot, mine, device).start()
        else:
            for slot, _, theirs, device in paired(k):
                copy(k, slot, theirs, device).wait_recv()

    def ring_end(k):
        copy(k, 0, block(k, core, color, "rest"), twin).wait_send()
        for slot, mine, _, device in (*inward(k), *paired(k)):
            copy(k, slot, mine, device).wait_send()

    def remote(src, dst, sems, slot, device):
        return pltpu.make_async_remote_copy(
            src_ref=src, dst_ref=dst, send_sem=sems[0].at[slot], recv_sem=sems[1].at[slot],
            device_id=device, device_id_type=MESH,
        )

    masks_out = [
        remote(mask_staged.at[pl.ds(1, 5)], mask_units.at[1, pl.ds(1, 5)], (mask_send, mask_recv), 0, west),
        remote(mask_staged.at[pl.ds(0, 1)], mask_units.at[1, pl.ds(6, 1)], (mask_send, mask_recv), 1, north_west),
        remote(mask_units.at[0, pl.ds(0, 1)], mask_units.at[0, pl.ds(6, 1)], (mask_send, mask_recv), 2, north),
    ]
    ahead = (ahead_send, ahead_recv)
    ahead_out = [
        [
            remote(staged.at[pl.ds(1, 1)], units.at[1, pl.ds(1, 1)], ahead, 0, west),
            remote(staged.at[pl.ds(0, 1)], units.at[1, pl.ds(6, 1)], ahead, 3, north_west),
            remote(units.at[0, pl.ds(0, 1)], units.at[0, pl.ds(6, 1)], ahead, 4, north),
        ],
        [remote(staged.at[pl.ds(2, 2)], units.at[1, pl.ds(2, 2)], ahead, 1, west)],
        [remote(staged.at[pl.ds(4, 2)], units.at[1, pl.ds(4, 2)], ahead, 2, west)],
    ]
    back = (back_send, back_recv)
    back_out = [
        [remote(returned.at[pl.ds(1, 2)], results.at[0, pl.ds(1, 2)], back, 0, east)],
        [remote(returned.at[pl.ds(3, 2)], results.at[0, pl.ds(3, 2)], back, 1, east)],
        [
            remote(returned.at[pl.ds(5, 1)], results.at[0, pl.ds(5, 1)], back, 2, east),
            remote(returned.at[pl.ds(6, 1)], results.at[0, pl.ds(0, 1)], back, 3, south_east),
            remote(results.at[1, pl.ds(6, 1)], results.at[1, pl.ds(0, 1)], back, 4, south),
        ],
    ]

    for k, step in PROLOGUE:
        ring(k, step)
        if (k, step) == PROLOGUE[0]:
            for c in masks_out:
                c.start()

    def at_points(point, table):
        for n, events in table.items():

            @pl.when(point == n)
            def _():
                for k, step in events:
                    ring(k, step)

    edge_row = (lat == n_lat - 1).astype(jnp.int32)

    for b in range(2):
        def gather_tokens(w):
            if b == 0:
                rows = pl.ds(pl.multiple_of(w * T, 16), T)
                code = code_ref[rows]
                xx[w, :T] = x_ref[rows]
                xx[w, T:] = (iota((T, D), 1) == lax.rem(code, D)).astype(BF)
                caps[w] = key_caps((code >= D).astype(F32), 0)
            else:

                @pl.when(w == 0)
                def _():
                    for c in (*masks_out, ahead_out[0][0], *ahead_out[1]):
                        c.wait_recv()

                @pl.when(w == 1)
                def _():
                    for c in ahead_out[2]:
                        c.wait_recv()

                @pl.when(w == 2)
                def _():
                    for c in ahead_out[0][1:]:
                        c.wait_recv()

                slots = pl.ds(2 * w + 1, 2)
                for s in range(2):
                    got = units[:, slots, s].reshape(4 * SLOT, D)
                    xx[w, s * T : (s + 1) * T] = dot(to_tokens[...], got).astype(BF)
                masks = mask_units[:, slots].reshape(4 * SLOT, 128)
                last = (w == WINDOWS - 1).astype(jnp.int32)
                caps[w] = key_caps(dot(to_tokens[...], masks)[:, :1], edge_row * last)

        def attend(w, half, point):
            if isinstance(half, int):
                if half == 0:
                    gather_tokens(w)
            else:

                @pl.when(half == 0)
                def _():
                    gather_tokens(w)

            project_qkv(xx[w], wa.at[b, half], pk)

            def pair(p, carry):
                head_pair(p, pk, caps.at[w], att.at[w, half])
                at_points(point + p, POINTS[b])
                return carry

            lax.fori_loop(0, 2, pair, 0)

        def expand(w, point):
            hb[...] = hid[w].astype(BF)

            def chunk(j, carry):
                up_chunk(j, hb, wb.at[b], act.at[w])
                at_points(point + j, POINTS[b])
                return carry

            lax.fori_loop(0, 4, chunk, 0)

        def contract(w):
            out = dot(act[w], wc[b].reshape(FF, D))
            n, dn = norm_pair(out[:T], out[T:])
            for s, grown in ((0, n), (1, dn)):
                final = (hid[w, s * T : (s + 1) * T] + grown).astype(BF)
                spread = dot(to_units[...], final).astype(BF).reshape(2, 2, SLOT, D)
                if b == 0:
                    staged[pl.ds(2 * w, 2), s] = spread[0]
                    units[0, pl.ds(2 * w, 2), s] = spread[1]
                else:
                    results[1, pl.ds(2 * w + 1, 2), s] = spread[0]
                    returned[pl.ds(2 * w + 1, 2), s] = spread[1]
            for i in range(WINDOWS):

                @pl.when(w == i)
                def _():
                    for c in (ahead_out, back_out)[b][i]:
                        c.start()

        def project(w):
            project_out(xx.at[w], att.at[w], wa.at[b], hid.at[w])

        def events(name):
            for k, step in NAMED[name]:
                ring(k, step)

        if b == 0:
            point = 0
            for group, (start, count) in enumerate(GROUPS):

                def attend_step(i, carry):
                    half = (i >= count).astype(jnp.int32)
                    if group == 0:

                        @pl.when(i == count)
                        def _():
                            events("second half")

                    attend(start + i - count * half, half, point + 2 * i)
                    return carry

                def project_step(i, carry):
                    project(start + i)
                    return carry

                def expand_step(i, carry):
                    expand(start + i, point + 4 * count + 4 * i)
                    return carry

                def contract_step(i, carry):
                    contract(start + i)
                    return carry

                lax.fori_loop(0, 2 * count, attend_step, 0)
                lax.fori_loop(0, count, project_step, 0)
                if group == 0:
                    events("first up")
                lax.fori_loop(0, count, expand_step, 0)
                if group == 0:
                    events("first down")
                lax.fori_loop(0, count, contract_step, 0)
                point += 8 * count
            events("second block")
        else:

            def window(w, carry):
                for half in range(2):
                    attend(w, half, 8 * w + 2 * half)
                project(w)

                @pl.when(w == 0)
                def _():
                    events("second up")

                expand(w, 8 * w + 4)

                @pl.when(w == 0)
                def _():
                    events("second down")

                contract(w)
                return carry

            lax.fori_loop(0, WINDOWS, window, 0)

    for w, waits in ((1, (*back_out[0], *back_out[1])), (2, back_out[2][:1]), (0, back_out[2][1:])):
        for c in waits:
            c.wait_recv()
        for s, out in ((0, out0), (1, out1)):
            got = results[:, 2 * w : 2 * w + 2, s].reshape(4 * SLOT, D)
            out[w * T : (w + 1) * T] = dot(to_tokens[...], got).astype(BF)
    for k in range(8):
        ring_end(k)
    for c in (*masks_out, *sum(ahead_out, []), *sum(back_out, [])):
        c.wait_send()


GROUPS = ((0, 3),)
PROLOGUE = ((0, 1), (1, 1), (2, 1), (0, 2), (3, 1), (1, 2), (0, 3), (0, 4))
POINTS = (
    {0: [(1, 3), (4, 1)], 1: [(5, 1)], 2: [(2, 2)], 3: [(6, 1)], 5: [(7, 1)], 8: [(3, 2)], 9: [(2, 3)],
     12: [(4, 2)], 14: [(3, 3), (5, 2)], 17: [(4, 3)], 19: [(6, 2)], 22: [(5, 3), (7, 2)]},
    {1: [(6, 3)], 4: [(7, 3)]},
)
NAMED = {
    "second half": ((1, 4),),
    "first up": ((2, 4),),
    "first down": ((3, 4),),
    "second block": ((4, 4), (5, 4)),
    "second up": ((6, 4),),
    "second down": ((7, 4),),
}


def on_device(fields, tangent_pick, key_mask, w_qkv, w_out, w_up, w_down):
    levels, rows, cols, _ = fields.shape
    tokens = levels * rows * cols
    x = jnp.transpose(fields, (1, 2, 0, 3)).reshape(tokens, D)
    code = jnp.transpose(tangent_pick + D * key_mask, (1, 2, 0)).reshape(tokens, 1)
    order = unit_order()
    to_tokens = jnp.asarray(order, BF)
    to_units = jnp.asarray(order.T, BF)
    vmem, hbm = pl.BlockSpec(memory_space=pltpu.VMEM), pl.BlockSpec(memory_space=pl.ANY)
    dma = pltpu.SemaphoreType.DMA
    outs = pl.pallas_call(
        kernel,
        out_shape=[jax.ShapeDtypeStruct((tokens, D), BF)] * 2,
        in_specs=[vmem] * 4 + [hbm] * 4,
        out_specs=[vmem] * 2,
        scratch_shapes=[
            pltpu.VMEM((2, 2, 32, 2 * D), BF),
            pltpu.VMEM((2, 32, FF), BF),
            pltpu.VMEM((2, 1, FF // 16, D), BF),
            pltpu.VMEM((2, 2, D, 2 * D), BF),
            pltpu.VMEM((2, D, FF), BF),
            pltpu.VMEM((2, 16, FF // 16, D), BF),
            pltpu.VMEM((2, 7, 2, SLOT, D), BF),
            pltpu.VMEM((6, 2, SLOT, D), BF),
            pltpu.VMEM((2, 7, 2, SLOT, D), BF),
            pltpu.VMEM((7, 2, SLOT, D), BF),
            pltpu.VMEM((2, 7, SLOT, 128), BF),
            pltpu.VMEM((6, SLOT, 128), BF),
            pltpu.VMEM((WINDOWS, 2 * T, D), BF),
            pltpu.VMEM((WINDOWS, 2 * T, D), F32),
            pltpu.VMEM((2 * T, D), BF),
            pltpu.VMEM((WINDOWS, 2 * T, FF), BF),
            pltpu.VMEM((2 * T, 768), BF),
            pltpu.VMEM((WINDOWS, 2, 2 * T, 256), BF),
            pltpu.VMEM((WINDOWS, T, 2 * T), F32),
            dma((20,)),
            dma((8,)),
            dma((8, 8)),
            dma((8, 8)),
            dma((3,)),
            dma((3,)),
            dma((5,)),
            dma((5,)),
            dma((5,)),
            dma((5,)),
        ],
        compiler_params=pltpu.CompilerParams(
            collective_id=0, has_side_effects=True, vmem_limit_bytes=52 * 1024 * 1024
        ),
        name="swin",
    )(x, code, to_tokens, to_units, w_qkv, w_out, w_up, w_down)
    return tuple(
        jnp.transpose(o.reshape(rows, cols, levels, D), (2, 0, 1, 3)) for o in outs
    )


def solution(mesh):
    weight = P(None, "lon", None)
    grid = P(None, "lat", "lon")
    field = P(None, "lat", "lon", None)
    return jax.shard_map(
        on_device,
        mesh=mesh,
        in_specs=(field, grid, grid, weight, weight, weight, weight),
        out_specs=(field, field),
        check_vma=False,
    )
```

time: 144 us -> 108 us (0.75)
  the two profiles are of different devices: /device:TPU:25 before, /device:TPU:64 now
where the time goes in v2:
time: 108 us; the launch traced here: 107 us
  Pallas kernels  102 us (94%)
  local copies, waits for them, and re-layouts  3.32 us (3%)
    pallas_call x1, Pallas kernels, on_device(): pl.pallas_call(kernel, out_shape=[jax.ShapeDtypeStruct((tokens, D), BF)]...  102 us

profile of v2, /device:TPU:64, one launch (start us, length us, event | category | flops | bytes accessed | tf_op | source)
XLA Modules:
  0.0 107.0 jit_solution(6683313743992521530)
XLA Ops:
  0.6 0.0 copy-start.6
  0.6 0.8 add_bitcast_fusion
  1.4 0.2 copy.12
  1.6 0.0 copy-start.4
  1.6 0.1 reshape.20.code_ref
  1.7 0.0 copy-done.6
  1.7 0.0 copy-start
  1.7 0.0 copy-start.1
  1.8 0.0 copy-start.2
  1.8 0.0 copy-start.3
  1.8 0.0 copy-start.5
  1.8 0.9 reshape.16.x_ref
  2.7 0.0 copy-done.4
  2.7 0.0 copy-done
  2.7 0.0 copy-done.1
  2.8 0.1 copy-done.2
  2.8 0.0 copy-done.3
  2.9 0.0 copy-done.5
  2.9 102.2 %swin.1 = (bf16[432,512]{1,0:T(8,128)(2,1)S(1)}, bf16[432,512]{1,0:T(8,128)(2,1)}) custom-call(bf16[432,512]{1,0:T(8,128)(2,1)} %reshape.16.x_ref, s32[432,1]{1,0:T(8,128)S(1)} %reshape.20.code_ref, bf16[144,192]{1,0:T(8,128)(2,1)S(1)} %copy-done.4, bf16[192,144]{1,0:T(8,128)(2,1)S(1)} %copy-done.3, bf16[2,32,1536]{2,1,0:T(8,128)(2,1)S(1)} %copy-done.2, ...), custom_call_target="tpu_custom_call" | custom-call | tf_op jit(solution)/shard_map/swin/pallas_call | solution.py:470
  105.1 0.0 copy-start.7
  105.1 0.9 reshape.18
  106.0 0.1 copy-done.7
  106.1 0.9 reshape.19
Async XLA Ops:
  0.6 1.1 %copy-start.6 = (bf16[2,18,12,512]{3,0,2,1:T(2,128)(2,1)S(1)}, bf16[2,18,12,512]{3,0,2,1:T(2,128)(2,1)}, u32[]{:S(2)}) copy-start(bf16[2,18,12,512]{3,0,2,1:T(2,128)(2,1)} %param.9) | copy-start | bytes 1327108
  1.6 1.1 %copy-start.4 = (bf16[144,192]{1,0:T(8,128)(2,1)S(1)}, bf16[144,192]{1,0:T(8,128)(2,1)}, u32[]{:S(2)}) copy-start(bf16[144,192]{1,0:T(8,128)(2,1)} %constant.6.clone.to_tokens) | copy-start | bytes 165892
  1.7 1.0 copy-start
  1.7 1.0 copy-start.1
  1.8 1.1 %copy-start.2 = (bf16[2,32,1536]{2,1,0:T(8,128)(2,1)S(1)}, bf16[2,32,1536]{2,1,0:T(8,128)(2,1)}, u32[]{:S(2)}) copy-start(bf16[2,32,1536]{2,1,0:T(8,128)(2,1)} %wqkv.1) | copy-start | bytes 589828
  1.8 1.1 %copy-start.3 = (bf16[192,144]{1,0:T(8,128)(2,1)S(1)}, bf16[192,144]{1,0:T(8,128)(2,1)}, u32[]{:S(2)}) copy-start(bf16[192,144]{1,0:T(8,128)(2,1)} %constant.7.clone.to_units) | copy-start | bytes 165892
  1.8 1.1 %copy-start.5 = (bf16[2,32,512]{2,1,0:T(8,128)(2,1)S(1)}, bf16[2,32,512]{2,1,0:T(8,128)(2,1)}, u32[]{:S(2)}) copy-start(bf16[2,32,512]{2,1,0:T(8,128)(2,1)} %wout.1) | copy-start | bytes 196612
  105.1 1.0 copy-start.7

commit v3 on v2

--- a/solution.py
+++ b/solution.py
@@ -245,15 +245,12 @@
         remote(mask_units.at[0, pl.ds(0, 1)], mask_units.at[0, pl.ds(6, 1)], (mask_send, mask_recv), 2, north),
     ]
     ahead = (ahead_send, ahead_recv)
-    ahead_out = [
-        [
-            remote(staged.at[pl.ds(1, 1)], units.at[1, pl.ds(1, 1)], ahead, 0, west),
-            remote(staged.at[pl.ds(0, 1)], units.at[1, pl.ds(6, 1)], ahead, 3, north_west),
-            remote(units.at[0, pl.ds(0, 1)], units.at[0, pl.ds(6, 1)], ahead, 4, north),
-        ],
-        [remote(staged.at[pl.ds(2, 2)], units.at[1, pl.ds(2, 2)], ahead, 1, west)],
-        [remote(staged.at[pl.ds(4, 2)], units.at[1, pl.ds(4, 2)], ahead, 2, west)],
+    ahead_west = [remote(staged.at[pl.ds(q, 1)], units.at[1, pl.ds(q, 1)], ahead, q - 1, west) for q in range(1, 6)]
+    ahead_north = [
+        remote(staged.at[pl.ds(0, 1)], units.at[1, pl.ds(6, 1)], ahead, 5, north_west),
+        remote(units.at[0, pl.ds(0, 1)], units.at[0, pl.ds(6, 1)], ahead, 6, north),
     ]
+    ahead_out = [ahead_west[:1], ahead_west[1:3], ahead_west[3:] + ahead_north]
     back = (back_send, back_recv)
     back_out = [
         [remote(returned.at[pl.ds(1, 2)], results.at[0, pl.ds(1, 2)], back, 0, east)],
@@ -265,11 +262,22 @@
         ],
     ]
 
-    for k, step in PROLOGUE:
+    for k, step in PROLOGUE[:3]:
         ring(k, step)
-        if (k, step) == PROLOGUE[0]:
-            for c in masks_out:
-                c.start()
+    for c in masks_out:
+        c.start()
+
+    def first_tokens(w, carry):
+        rows = pl.ds(pl.multiple_of(w * T, 16), T)
+        code = code_ref[rows]
+        xx[w, :T] = x_ref[rows]
+        xx[w, T:] = (iota((T, D), 1) == lax.rem(code, D)).astype(BF)
+        caps[w] = key_caps((code >= D).astype(F32), 0)
+        return carry
+
+    lax.fori_loop(0, WINDOWS, first_tokens, 0)
+    for k, step in PROLOGUE[3:]:
+        ring(k, step)
 
     def at_points(point, table):
         for n, events in table.items():
@@ -283,47 +291,25 @@
 
     for b in range(2):
         def gather_tokens(w):
-            if b == 0:
-                rows = pl.ds(pl.multiple_of(w * T, 16), T)
-                code = code_ref[rows]
-                xx[w, :T] = x_ref[rows]
-                xx[w, T:] = (iota((T, D), 1) == lax.rem(code, D)).astype(BF)
-                caps[w] = key_caps((code >= D).astype(F32), 0)
-            else:
-
-                @pl.when(w == 0)
+            needed = (masks_out + ahead_west[:2], ahead_west[2:4], ahead_west[4:] + ahead_north)
+            for i in range(WINDOWS):
+
+                @pl.when(w == i)
                 def _():
-                    for c in (*masks_out, ahead_out[0][0], *ahead_out[1]):
+                    for c in needed[i]:
                         c.wait_recv()
 
-                @pl.when(w == 1)
-                def _():
-                    for c in ahead_out[2]:
-                        c.wait_recv()
-
-                @pl.when(w == 2)
-                def _():
-                    for c in ahead_out[0][1:]:
-                        c.wait_recv()
-
-                slots = pl.ds(2 * w + 1, 2)
-                for s in range(2):
-                    got = units[:, slots, s].reshape(4 * SLOT, D)
-                    xx[w, s * T : (s + 1) * T] = dot(to_tokens[...], got).astype(BF)
-                masks = mask_units[:, slots].reshape(4 * SLOT, 128)
-                last = (w == WINDOWS - 1).astype(jnp.int32)
-                caps[w] = key_caps(dot(to_tokens[...], masks)[:, :1], edge_row * last)
+            slots = pl.ds(2 * w + 1, 2)
+            for s in range(2):
+                got = units[:, slots, s].reshape(4 * SLOT, D)
+                xx[w, s * T : (s + 1) * T] = dot(to_tokens[...], got).astype(BF)
+            masks = mask_units[:, slots].reshape(4 * SLOT, 128)
+            last = (w == WINDOWS - 1).astype(jnp.int32)
+            caps[w] = key_caps(dot(to_tokens[...], masks)[:, :1], edge_row * last)
 
         def attend(w, half, point):
-            if isinstance(half, int):
-                if half == 0:
-                    gather_tokens(w)
-            else:
-
-                @pl.when(half == 0)
-                def _():
-                    gather_tokens(w)
-
+            if b == 1 and half == 0:
+                gather_tokens(w)
             project_qkv(xx[w], wa.at[b, half], pk)
 
             def pair(p, carry):
@@ -443,16 +429,16 @@
 GROUPS = ((0, 3),)
 PROLOGUE = ((0, 1), (1, 1), (2, 1), (0, 2), (3, 1), (1, 2), (0, 3), (0, 4))
 POINTS = (
-    {0: [(1, 3), (4, 1)], 1: [(5, 1)], 2: [(2, 2)], 3: [(6, 1)], 5: [(7, 1)], 8: [(3, 2)], 9: [(2, 3)],
-     12: [(4, 2)], 14: [(3, 3), (5, 2)], 17: [(4, 3)], 19: [(6, 2)], 22: [(5, 3), (7, 2)]},
-    {1: [(6, 3)], 4: [(7, 3)]},
+    {0: [(1, 3), (4, 1)], 1: [(2, 2), (5, 1)], 2: [(6, 1)], 4: [(7, 1)], 5: [(3, 2)], 6: [(2, 3)], 8: [(4, 2)], 10: [(5, 2)],
+     11: [(3, 3)], 13: [(4, 3)], 15: [(6, 2)], 17: [(5, 3)], 19: [(7, 2)], 21: [(6, 3)]},
+    {0: [(7, 3)]},
 )
 NAMED = {
     "second half": ((1, 4),),
     "first up": ((2, 4),),
     "first down": ((3, 4),),
-    "second block": ((4, 4), (5, 4)),
-    "second up": ((6, 4),),
+    "second block": ((4, 4), (5, 4), (6, 4)),
+    "second up": (),
     "second down": ((7, 4),),
 }
 
@@ -498,8 +484,8 @@
             dma((8, 8)),
             dma((3,)),
             dma((3,)),
-            dma((5,)),
-            dma((5,)),
+            dma((7,)),
+            dma((7,)),
             dma((5,)),
             dma((5,)),
         ],

time: 108 us -> 102 us (0.944); the launches traced: 107 us -> 102 us
  Pallas kernels: 102 us -> 97.3 us
    pallas_call x1, Pallas kernels: 102 us -> 97.3 us  [on_device(): pl.pallas_call(kernel, out_shape=[jax.ShapeDtypeStruct((tokens, D), BF)]...]
where the time goes in v3:
time: 102 us
  Pallas kernels  97.3 us (95%)
  local copies, waits for them, and re-layouts  3.32 us (3%)
    pallas_call x1, Pallas kernels, on_device(): pl.pallas_call(kernel, out_shape=[jax.ShapeDtypeStruct((tokens, D), BF)]...  97.3 us

profile of v3, /device:TPU:64, one launch (start us, length us, event | category | flops | bytes accessed | tf_op | source)
XLA Modules:
  0.0 102.2 jit_solution(1946657795313522537)
XLA Ops:
  0.6 0.0 copy-start.6
  0.6 0.8 add_bitcast_fusion
  1.4 0.2 copy.12
  1.6 0.0 copy-start.4
  1.6 0.1 reshape.20.code_ref
  1.7 0.0 copy-done.6
  1.7 0.0 copy-start
  1.7 0.0 copy-start.1
  1.8 0.0 copy-start.2
  1.8 0.0 copy-start.3
  1.8 0.0 copy-start.5
  1.8 0.9 reshape.16.x_ref
  2.7 0.0 copy-done.4
  2.7 0.0 copy-done
  2.7 0.0 copy-done.1
  2.8 0.1 copy-done.2
  2.8 0.0 copy-done.3
  2.9 0.0 copy-done.5
  2.9 97.3 %swin.1 = (bf16[432,512]{1,0:T(8,128)(2,1)S(1)}, bf16[432,512]{1,0:T(8,128)(2,1)}) custom-call(bf16[432,512]{1,0:T(8,128)(2,1)} %reshape.16.x_ref, s32[432,1]{1,0:T(8,128)S(1)} %reshape.20.code_ref, bf16[144,192]{1,0:T(8,128)(2,1)S(1)} %copy-done.4, bf16[192,144]{1,0:T(8,128)(2,1)S(1)} %copy-done.3, bf16[2,32,1536]{2,1,0:T(8,128)(2,1)S(1)} %copy-done.2, ...), custom_call_target="tpu_custom_call" | custom-call | tf_op jit(solution)/shard_map/swin/pallas_call | solution.py:456
  100.2 0.0 copy-start.7
  100.2 0.9 reshape.18
  101.2 0.1 copy-done.7
  101.2 0.9 reshape.19
Async XLA Ops:
  0.6 1.1 %copy-start.6 = (bf16[2,18,12,512]{3,0,2,1:T(2,128)(2,1)S(1)}, bf16[2,18,12,512]{3,0,2,1:T(2,128)(2,1)}, u32[]{:S(2)}) copy-start(bf16[2,18,12,512]{3,0,2,1:T(2,128)(2,1)} %param.9) | copy-start | bytes 1327108
  1.6 1.1 %copy-start.4 = (bf16[144,192]{1,0:T(8,128)(2,1)S(1)}, bf16[144,192]{1,0:T(8,128)(2,1)}, u32[]{:S(2)}) copy-start(bf16[144,192]{1,0:T(8,128)(2,1)} %constant.6.clone.to_tokens) | copy-start | bytes 165892
  1.7 1.0 copy-start
  1.7 1.0 %copy-start.1 = (bf16[2,128,512]{2,1,0:T(8,128)(2,1)S(1)}, bf16[2,128,512]{2,1,0:T(8,128)(2,1)}, u32[]{:S(2)}) copy-start(bf16[2,128,512]{2,1,0:T(8,128)(2,1)} %wdown.1) | copy-start | bytes 786436
  1.8 1.1 %copy-start.2 = (bf16[2,32,1536]{2,1,0:T(8,128)(2,1)S(1)}, bf16[2,32,1536]{2,1,0:T(8,128)(2,1)}, u32[]{:S(2)}) copy-start(bf16[2,32,1536]{2,1,0:T(8,128)(2,1)} %wqkv.1) | copy-start | bytes 589828
  1.8 1.1 %copy-start.3 = (bf16[192,144]{1,0:T(8,128)(2,1)S(1)}, bf16[192,144]{1,0:T(8,128)(2,1)}, u32[]{:S(2)}) copy-start(bf16[192,144]{1,0:T(8,128)(2,1)} %constant.7.clone.to_units) | copy-start | bytes 165892
  1.8 1.1 %copy-start.5 = (bf16[2,32,512]{2,1,0:T(8,128)(2,1)S(1)}, bf16[2,32,512]{2,1,0:T(8,128)(2,1)}, u32[]{:S(2)}) copy-start(bf16[2,32,512]{2,1,0:T(8,128)(2,1)} %wout.1) | copy-start | bytes 196612
  100.2 1.0 copy-start.7

commit v4 on v3

--- a/solution.py
+++ b/solution.py
@@ -312,22 +312,22 @@
                 gather_tokens(w)
             project_qkv(xx[w], wa.at[b, half], pk)
 
-            def pair(p, carry):
+            for p in range(2):
                 head_pair(p, pk, caps.at[w], att.at[w, half])
+            for p in range(2):
                 at_points(point + p, POINTS[b])
-                return carry
-
-            lax.fori_loop(0, 2, pair, 0)
 
         def expand(w, point):
             hb[...] = hid[w].astype(BF)
 
-            def chunk(j, carry):
-                up_chunk(j, hb, wb.at[b], act.at[w])
-                at_points(point + j, POINTS[b])
+            def chunks(i, carry):
+                for j in range(2):
+                    up_chunk(2 * i + j, hb, wb.at[b], act.at[w])
+                for j in range(2):
+                    at_points(point + 2 * i + j, POINTS[b])
                 return carry
 
-            lax.fori_loop(0, 4, chunk, 0)
+            lax.fori_loop(0, 2, chunks, 0)
 
         def contract(w):
             out = dot(act[w], wc[b].reshape(FF, D))

time: 102 us -> 98.8 us (0.969)
  Pallas kernels: 97.3 us -> 93.8 us
    pallas_call x1, Pallas kernels: 97.3 us -> 93.8 us  [on_device(): pl.pallas_call(kernel, out_shape=[jax.ShapeDtypeStruct((tokens, D), BF)]...]
where the time goes in v4:
time: 98.8 us; the launch traced here: 98.6 us
  Pallas kernels  93.8 us (95%)
  local copies, waits for them, and re-layouts  3.32 us (3%)
    pallas_call x1, Pallas kernels, on_device(): pl.pallas_call(kernel, out_shape=[jax.ShapeDtypeStruct((tokens, D), BF)]...  93.8 us

profile of v4, /device:TPU:64, one launch (start us, length us, event | category | flops | bytes accessed | tf_op | source)
XLA Modules:
  0.0 98.6 jit_solution(6729289310544867053)
XLA Ops:
  0.6 0.0 copy-start.6
  0.6 0.8 add_bitcast_fusion
  1.4 0.2 copy.12
  1.6 0.0 copy-start.4
  1.6 0.1 reshape.20.code_ref
  1.7 0.0 copy-done.6
  1.7 0.0 copy-start
  1.7 0.0 copy-start.1
  1.8 0.0 copy-start.2
  1.8 0.0 copy-start.3
  1.8 0.0 copy-start.5
  1.8 0.9 reshape.16.x_ref
  2.7 0.0 copy-done.4
  2.7 0.0 copy-done
  2.7 0.0 copy-done.1
  2.8 0.1 copy-done.2
  2.8 0.0 copy-done.3
  2.9 0.0 copy-done.5
  2.9 93.8 %swin.1 = (bf16[432,512]{1,0:T(8,128)(2,1)S(1)}, bf16[432,512]{1,0:T(8,128)(2,1)}) custom-call(bf16[432,512]{1,0:T(8,128)(2,1)} %reshape.16.x_ref, s32[432,1]{1,0:T(8,128)S(1)} %reshape.20.code_ref, bf16[144,192]{1,0:T(8,128)(2,1)S(1)} %copy-done.4, bf16[192,144]{1,0:T(8,128)(2,1)S(1)} %copy-done.3, bf16[2,32,1536]{2,1,0:T(8,128)(2,1)S(1)} %copy-done.2, ...), custom_call_target="tpu_custom_call" | custom-call | tf_op jit(solution)/shard_map/swin/pallas_call | solution.py:456
  96.7 0.0 copy-start.7
  96.7 0.9 reshape.18
  97.6 0.1 copy-done.7
  97.7 0.9 reshape.19
Async XLA Ops:
  0.6 1.1 %copy-start.6 = (bf16[2,18,12,512]{3,0,2,1:T(2,128)(2,1)S(1)}, bf16[2,18,12,512]{3,0,2,1:T(2,128)(2,1)}, u32[]{:S(2)}) copy-start(bf16[2,18,12,512]{3,0,2,1:T(2,128)(2,1)} %param.9) | copy-start | bytes 1327108
  1.6 1.1 %copy-start.4 = (bf16[144,192]{1,0:T(8,128)(2,1)S(1)}, bf16[144,192]{1,0:T(8,128)(2,1)}, u32[]{:S(2)}) copy-start(bf16[144,192]{1,0:T(8,128)(2,1)} %constant.6.clone.to_tokens) | copy-start | bytes 165892
  1.7 1.0 %copy-start = (bf16[2,32,2048]{2,1,0:T(8,128)(2,1)S(1)}, bf16[2,32,2048]{2,1,0:T(8,128)(2,1)}, u32[]{:S(2)}) copy-start(bf16[2,32,2048]{2,1,0:T(8,128)(2,1)} %wup.1) | copy-start | bytes 786436
  1.7 1.0 %copy-start.1 = (bf16[2,128,512]{2,1,0:T(8,128)(2,1)S(1)}, bf16[2,128,512]{2,1,0:T(8,128)(2,1)}, u32[]{:S(2)}) copy-start(bf16[2,128,512]{2,1,0:T(8,128)(2,1)} %wdown.1) | copy-start | bytes 786436
  1.8 1.1 %copy-start.2 = (bf16[2,32,1536]{2,1,0:T(8,128)(2,1)S(1)}, bf16[2,32,1536]{2,1,0:T(8,128)(2,1)}, u32[]{:S(2)}) copy-start(bf16[2,32,1536]{2,1,0:T(8,128)(2,1)} %wqkv.1) | copy-start | bytes 589828
  1.8 1.1 %copy-start.3 = (bf16[192,144]{1,0:T(8,128)(2,1)S(1)}, bf16[192,144]{1,0:T(8,128)(2,1)}, u32[]{:S(2)}) copy-start(bf16[192,144]{1,0:T(8,128)(2,1)} %constant.7.clone.to_units) | copy-start | bytes 165892
  1.8 1.1 %copy-start.5 = (bf16[2,32,512]{2,1,0:T(8,128)(2,1)S(1)}, bf16[2,32,512]{2,1,0:T(8,128)(2,1)}, u32[]{:S(2)}) copy-start(bf16[2,32,512]{2,1,0:T(8,128)(2,1)} %wout.1) | copy-start | bytes 196612
  96.7 1.0 %copy-start.7 = (bf16[432,512]{1,0:T(8,128)(2,1)S(1)}, bf16[432,512]{1,0:T(8,128)(2,1)}, u32[]{:S(2)}) copy-start(bf16[432,512]{1,0:T(8,128)(2,1)} %get-tuple-element.5) | copy-start | bytes 1327108
